TPU v7x, 512 devices: a whole 4x4x16 slice. The times are simulated.
512 devices in a mesh: dp: 128 (over x, z, core), mp: 4 (over y).
Axes of the slice: x: 4, y: 4, z: 16, core: 2. Of those that a mesh axis runs over, the one named last changes fastest.
Arguments:
- patches: bfloat16 [32768, 1280], P('dp', 'mp'), may hold values from -6 to 6
- routes: int32 [32768, 1], P('dp'), may hold values from 0 to 127; in each aligned block of 256 rows (0 to 255, 256 to 511, ...) at most 4 rows name the same one
- gain: bfloat16 [1280], replicated, may hold values from 0.099609375 to 1.8984375
- shift: bfloat16 [1280], replicated, may hold values from -2 to 2
- first_weight: bfloat16 [1280, 5120], P('dp', 'mp'), may hold values from -0.15625 to 0.15625
- first_bias: bfloat16 [5120], P('mp'), may hold values from -3 to 3
- adapter_down: bfloat16 [1280, 64], replicated, may hold values from -0.15625 to 0.15625
- adapter_up: bfloat16 [64, 5120], P(None, 'mp'), may hold values from -0.75 to 0.75
- second_weight: bfloat16 [5120, 1280], P('mp', 'dp'), may hold values from -0.078125 to 0.078125
- second_bias: bfloat16 [1280], P('mp'), may hold values from -3 to 3
- language_slot_gradient: bfloat16 [65536, 1280], P('dp', 'mp'), may hold values from -6 to 6
Outputs:
- embeds_llm: bfloat16 [65536, 1280], P('dp', 'mp')
- grad_lora_a: float32 [1280, 64], replicated
- grad_lora_b: float32 [64, 5120], P(None, 'mp')
Inputs may be any that keep to these rules, and one draw needn't show every extreme that they name: `routes`: among the rows of one data rank, no destination is named more than 4 times, a bound that some block reaches.
All inputs are finite; a program needn't handle non-finite values.
Results may differ from a plain program's by a relative error of at most 0.012.
Values may be sent and summed in bfloat16 or wider, within the bound.
A program may use at most 64 MiB of HBM per device.

v0:
```python
import math

import jax
import jax.numpy as jnp
from jax import lax
from jax.sharding import PartitionSpec as P


def quick_gelu(values):
    return values * jax.nn.sigmoid(1.702 * values)


def gelu_slope(values):
    sigma = jax.nn.sigmoid(1.702 * values)
    return sigma + 1.702 * values * sigma * (1.0 - sigma)


def normalize(patch_rows, gain, shift):
    floats = patch_rows.astype(jnp.float32)
    row_mean = jnp.mean(floats, axis=-1, keepdims=True)
    centred = floats - row_mean
    row_var = jnp.mean(centred * centred, axis=-1, keepdims=True)
    scaled = centred * lax.rsqrt(row_var + 1e-06) * gain.astype(jnp.float32) + shift.astype(
        jnp.float32
    )
    return scaled.astype(jnp.bfloat16)


def local(
    patches,
    routes,
    gain,
    shift,
    first_weight,
    first_bias,
    adapter_down,
    adapter_up,
    second_weight,
    second_bias,
    language_slot_gradient,
):
    rank_count = lax.axis_size("dp")
    row_count = patches.shape[0]
    capacity = language_slot_gradient.shape[0] // rank_count
    destination = routes[:, 0]
    hit_table = (destination[:, None] == jnp.arange(rank_count, dtype=jnp.int32)[None, :]).astype(
        jnp.int32
    )
    before = jnp.cumsum(hit_table, axis=0) - hit_table
    rank_in = jnp.sum(before * hit_table, axis=1)
    slot_of = destination * capacity + rank_in
    placing = (
        slot_of[None, :] == jnp.arange(rank_count * capacity, dtype=jnp.int32)[:, None]
    ).astype(jnp.bfloat16)
    returned = lax.all_to_all(language_slot_gradient, "dp", split_axis=0, concat_axis=0, tiled=True)
    grad_local = lax.dot_general(
        placing, returned, (((0,), (0,)), ((), ())), preferred_element_type=jnp.float32
    ).astype(jnp.bfloat16)
    whole_rows = lax.all_gather(patches, "mp", axis=1, tiled=True)
    normalized_rows = normalize(whole_rows, gain, shift)
    adapter_latent = jnp.dot(
        normalized_rows, adapter_down, preferred_element_type=jnp.float32
    ).astype(jnp.bfloat16)
    first_full, second_full = (
        lax.all_gather(first_weight, "dp", axis=0, tiled=True),
        lax.all_gather(second_weight, "dp", axis=1, tiled=True),
    )
    pre_main = jnp.dot(normalized_rows, first_full, preferred_element_type=jnp.float32)
    preactivation = (
        pre_main
        + jnp.dot(adapter_latent, adapter_up, preferred_element_type=jnp.float32)
        + first_bias.astype(jnp.float32)
    )
    activated = quick_gelu(preactivation).astype(jnp.bfloat16)
    partial_out = jnp.dot(activated, second_full, preferred_element_type=jnp.float32)
    branch_out = lax.psum_scatter(
        partial_out.astype(jnp.bfloat16), "mp", scatter_dimension=1, tiled=True
    ).astype(jnp.float32)
    embeds = (patches.astype(jnp.float32) + branch_out + second_bias.astype(jnp.float32)).astype(
        jnp.bfloat16
    )
    outgoing = jnp.dot(placing, embeds, preferred_element_type=jnp.float32).astype(jnp.bfloat16)
    embeds_llm = lax.all_to_all(outgoing, "dp", split_axis=0, concat_axis=0, tiled=True)
    whole_grad = lax.all_gather(grad_local, "mp", axis=1, tiled=True)
    grad_act = lax.dot_general(
        whole_grad, second_full, (((1,), (1,)), ((), ())), preferred_element_type=jnp.float32
    )
    preactivation_gradient = (grad_act * gelu_slope(preactivation)).astype(jnp.bfloat16)
    adapter_gradient = lax.dot_general(
        preactivation_gradient,
        adapter_up,
        (((1,), (1,)), ((), ())),
        preferred_element_type=jnp.float32,
    )
    grad_b_part = lax.dot_general(
        adapter_latent,
        preactivation_gradient,
        (((0,), (0,)), ((), ())),
        preferred_element_type=jnp.float32,
    )
    normalized_wide = normalized_rows.astype(jnp.float32)
    grad_scale = 1.0 / math.sqrt(row_count * rank_count)
    grad_a_part = lax.dot_general(
        normalized_wide, adapter_gradient, (((0,), (0,)), ((), ())), precision=lax.Precision.HIGHEST
    )
    down_gradient = lax.psum(grad_a_part, ("dp", "mp"))
    grad_b = lax.psum(grad_b_part, "dp")
    return (embeds_llm, down_gradient * grad_scale, grad_b * grad_scale)


def solution(mesh):
    placed = (
        P("dp", "mp"),
        P("dp", None),
        P(),
        P(),
        P("dp", "mp"),
        P("mp"),
        P(),
        P(None, "mp"),
        P("mp", "dp"),
        P("mp"),
        P("dp", "mp"),
    )
    return jax.shard_map(
        local,
        mesh=mesh,
        in_specs=placed,
        out_specs=(P("dp", "mp"), P(), P(None, "mp")),
        check_vma=False,
    )
```

profile of v0, /device:TPU:1, one launch (start us, length us, event | category | flops | bytes accessed | tf_op | source)
XLA Modules:
  0.0 1169.0 jit_solution(4410420905834089916)
XLA Ops:
  7.2 0.0 copy-start
  7.2 0.0 copy-start.5
  7.2 0.0 copy-start.6
  7.2 0.0 copy-start.7
  7.2 0.0 copy-start.4
  7.2 0.0 all-gather.5.cloned.1.call-start
  7.3 0.7 all-gather.5.cloned.1.call-update
  8.0 0.0 all-gather.7.cloned.1.call-start
  8.0 0.7 all-gather.7.cloned.1.call-update
  8.7 1.2 copy.23
  9.9 0.0 copy-start.3
  9.9 0.9 all_to_all.19
  10.8 20.4 %all-to-all-start.1 = ((bf16[128,4,320]{2,1,0:T(4,128)(2,1)}), bf16[128,4,320]{2,1,0:T(4,128)(2,1)S(1)}, u32[]{:S(2)}, u32[]{:S(2)}) async-start(bf16[128,4,320]{2,1,0:T(4,128)(2,1)} %all_to_all.19), calls=%async_computation.2 | async-start | bytes 786432 | tf_op jit(solution)/shard_map/all_to_all | solution.py:55
  31.2 0.0 reduce-scatter.2.cloned.1.call-start
  31.2 0.0 copy-done.5
  31.2 0.0 copy-done.6
  31.3 0.0 copy-done.7
  31.3 0.0 copy-done.4
  31.3 0.1 copy.20
  31.4 0.2 fusion.13
  31.7 0.2 fusion.15
  31.9 0.0 copy-done.3
  31.9 12.5 %all_gather.12 = bf16[256,1280]{0,1:T(8,128)(2,1)S(1)} all-gather(bf16[256,320]{0,1:T(8,128)(2,1)S(1)} %copy-done.3), channel_id=1, replica_groups=mesh['dp'=128,'mp'=4] {'mp'}, dimensions={1}, use_global_device_ids=true | all-gather | bytes 819200 | tf_op jit(solution)/shard_map/all_gather | solution.py:59
  44.4 0.2 convert_reduce_fusion
  44.6 0.2 fusion.4
  44.9 0.4 fusion.7
  45.3 0.1 copy-done.2
  45.4 0.2 convolution_convert_fusion.3
  45.6 115.5 %all-gather.5.cloned.1.call-done = bf16[128,10,1280]{2,1,0:T(8,128)(2,1)} async-done(((bf16[1,10,1280]{2,1,0:T(8,128)(2,1)}), bf16[128,10,1280]{2,1,0:T(8,128)(2,1)}) %all-gather.5.cloned.1.call-update) | async-done | bytes 3276816 | tf_op jit(solution)/shard_map/all_gather | solution.py:65
  161.1 7.0 reshape.52
  168.2 134.8 %all-gather.7.cloned.1.call-done = bf16[128,10,1280]{2,1,0:T(8,128)(2,1)} async-done(((bf16[1,10,1280]{2,1,0:T(8,128)(2,1)}), bf16[128,10,1280]{2,1,0:T(8,128)(2,1)}) %all-gather.7.cloned.1.call-update) | async-done | bytes 3276816 | tf_op jit(solution)/shard_map/all_gather | solution.py:66
  302.9 7.1 reshape.54
  310.0 3.1 fusion.20
  313.1 0.0 copy-done
  313.1 0.4 fusion
  313.5 0.0 copy-done.1
  313.5 0.0 copy-start.8
  313.5 2.0 convolution_convert_fusion
  315.5 0.0 reduce-scatter.2.cloned.1.call-update
  315.6 0.0 copy-done.8
  315.6 0.0 all-to-all-done.1
  315.6 0.2 all_to_all.21
  315.8 0.3 convolution_convert_fusion.2
  316.1 11.6 all_gather.15
  327.7 3.2 fusion.1
  330.9 0.3 fusion.21
  331.2 7.7 reduce-scatter.2.cloned.1.call-done
  339.0 1.2 convolution_convert_fusion.1
  340.2 0.2 copy.22
  340.4 0.9 all_to_all.16
  341.3 17.7 %all-to-all-start = ((bf16[128,4,320]{2,1,0:T(4,128)(2,1)}), bf16[128,4,320]{2,1,0:T(4,128)(2,1)S(1)}, u32[]{:S(2)}, u32[]{:S(2)}) async-start(bf16[128,4,320]{2,1,0:T(4,128)(2,1)} %all_to_all.16), calls=%async_computation.1 | async-start | bytes 786432 | tf_op jit(solution)/shard_map/all_to_all | solution.py:83
  359.0 0.0 all-reduce.3.cloned.1.call-start
  359.1 1.5 fusion.22
  360.5 0.0 all-reduce.3.cloned.1.call-update
  360.5 0.0 all-reduce.5.cloned.1.call-start
  360.6 1.0 fusion.23
  361.6 0.0 all-reduce.5.cloned.1.call-update
  361.6 464.5 %all-reduce.3.cloned.1.call-done = f32[1280,64]{0,1:T(8,128)} async-done(((f32[1280,64]{0,1:T(8,128)}), f32[1280,64]{0,1:T(8,128)}) %all-reduce.3.cloned.1.call-update) | async-done | bytes 327696 | tf_op jit(solution)/shard_map/psum | solution.py:106
  826.0 1.7 broadcast_multiply_fusion.1
  827.8 331.9 %all-reduce.5.cloned.1.call-done = f32[64,1280]{1,0:T(8,128)} async-done(((f32[64,1280]{1,0:T(8,128)}), f32[64,1280]{1,0:T(8,128)}) %all-reduce.5.cloned.1.call-update) | async-done | bytes 327696 | tf_op jit(solution)/shard_map/psum | solution.py:107
  1159.7 1.7 broadcast_multiply_fusion
  1161.4 0.0 all-to-all-done
  1161.4 0.2 all_to_all.18
  1161.6 0.9 copy.24
  (15 shorter events, 0.1 us)
Async XLA Ops:
  7.2 306.0 %copy-start = (bf16[64,1280]{1,0:T(8,128)(2,1)S(1)}, bf16[64,1280]{1,0:T(8,128)(2,1)}, u32[]{:S(2)}) copy-start(bf16[64,1280]{1,0:T(8,128)(2,1)} %param.18) | copy-start | bytes 491524
  7.2 24.0 %copy-start.5 = (bf16[1280]{0:T(1024)(128)(2,1)S(1)}, bf16[1280]{0:T(1024)(128)(2,1)}, u32[]{:S(2)}) copy-start(bf16[1280]{0:T(1024)(128)(2,1)} %param.13) | copy-start | bytes 7684
  7.2 24.0 %copy-start.6 = (bf16[1280]{0:T(1024)(128)(2,1)S(1)}, bf16[1280]{0:T(1024)(128)(2,1)}, u32[]{:S(2)}) copy-start(bf16[1280]{0:T(1024)(128)(2,1)} %param.14) | copy-start | bytes 7684
  7.2 24.1 %copy-start.7 = (bf16[1280]{0:T(1024)(128)(2,1)S(1)}, bf16[1280]{0:T(1024)(128)(2,1)}, u32[]{:S(2)}) copy-start(bf16[1280]{0:T(1024)(128)(2,1)} %param.16) | copy-start | bytes 7684
  7.2 24.1 %copy-start.4 = (s32[256,1]{0,1:T(1,128)S(1)}, s32[256,1]{0,1:T(1,128)}, u32[]{:S(2)}) copy-start(s32[256,1]{0,1:T(1,128)} %param.12) | copy-start | bytes 3076
  7.2 153.9 %all-gather.5.cloned.1.call-start = ((), (), s32[]{:S(2)}) async-start(), calls=%async_computation.6 | async-start | bytes 5283840 | tf_op jit(solution)/shard_map/all_gather | solution.py:65
  8.0 295.0 %all-gather.7.cloned.1.call-start = ((), (), s32[]{:S(2)}) async-start(), calls=%async_computation.7 | async-start | bytes 5283840 | tf_op jit(solution)/shard_map/all_gather | solution.py:66
  9.9 22.0 %copy-start.3 = (bf16[256,320]{0,1:T(8,128)(2,1)S(1)}, bf16[256,320]{0,1:T(8,128)(2,1)}, u32[]{:S(2)}) copy-start(bf16[256,320]{0,1:T(8,128)(2,1)} %param.11) | copy-start | bytes 491524
  10.8 304.8 %all-to-all-start.1 = ((bf16[128,4,320]{2,1,0:T(4,128)(2,1)}), bf16[128,4,320]{2,1,0:T(4,128)(2,1)S(1)}, u32[]{:S(2)}, u32[]{:S(2)}) async-start(bf16[128,4,320]{2,1,0:T(4,128)(2,1)} %all_to_all.19), calls=%async_computation.2 | async-start | bytes 786432 | tf_op jit(solution)/shard_map/all_to_all | solution.py:55
  31.2 307.8 %reduce-scatter.2.cloned.1.call-start = ((), (), s32[]{:S(2)}) async-start(), calls=%async_computation.3 | async-start | bytes 819200 | tf_op jit(solution)/shard_map/reduce_scatter | solution.py:76
  44.4 0.9 copy-start.2
  310.0 3.5 copy-start.1
  313.5 2.1 copy-start.8
  341.3 820.1 %all-to-all-start = ((bf16[128,4,320]{2,1,0:T(4,128)(2,1)}), bf16[128,4,320]{2,1,0:T(4,128)(2,1)S(1)}, u32[]{:S(2)}, u32[]{:S(2)}) async-start(bf16[128,4,320]{2,1,0:T(4,128)(2,1)} %all_to_all.16), calls=%async_computation.1 | async-start | bytes 786432 | tf_op jit(solution)/shard_map/all_to_all | solution.py:83
  359.0 467.0 %all-reduce.3.cloned.1.call-start = ((), (), s32[]{:S(2)}) async-start(), calls=%async_computation.4 | async-start | bytes 655360 | tf_op jit(solution)/shard_map/psum | solution.py:106
  360.5 799.1 %all-reduce.5.cloned.1.call-start = ((), (), s32[]{:S(2)}) async-start(), calls=%async_computation.5 | async-start | bytes 655360 | tf_op jit(solution)/shard_map/psum | solution.py:107
Sparse Core Ops, SparseCore 0:
  11.2 149.9 all-gather.4
  164.3 138.6 all-gather.6
  315.7 23.2 reduce-scatter.1
  365.5 460.4 all-reduce.2
  830.3 329.3 all-reduce.4
where the time goes:
time: 1170 us
  waiting for transfers between devices  1060 us (91%)
  starting transfers between devices  38.3 us (3%)
  blocking collectives  24.1 us (2%)
  local copies, waits for them, and re-layouts  18.7 us (2%)
  between operations  14.1 us (1%)
  matrix products  13.2 us (1%)
    psum x1, waiting for transfers between devices, local(): down_gradient = lax.psum(grad_a_part, ('dp', 'mp'))  464 us
    psum x1, waiting for transfers between devices, local(): grad_b = lax.psum(grad_b_part, 'dp')  332 us
    all_gather x1, waiting for transfers between devices, local(): lax.all_gather(second_weight, 'dp', axis=1, tiled=True)  135 us
    all_gather x1, waiting for transfers between devices, local(): lax.all_gather(first_weight, 'dp', axis=0, tiled=True)  116 us
  transfers between devices with their start and end apart: 7, of which 5 were waited for; matrix products, arithmetic and copies ran while one was open for 3% of the time, Pallas kernels for 0%

commit v1 on v0

--- a/solution.py
+++ b/solution.py
@@ -98,14 +98,46 @@
         (((0,), (0,)), ((), ())),
         preferred_element_type=jnp.float32,
     )
-    normalized_wide = normalized_rows.astype(jnp.float32)
     grad_scale = 1.0 / math.sqrt(row_count * rank_count)
+    adapter_gradient = jnp.sum(lax.all_gather(adapter_gradient, "mp", axis=0), axis=0)
+    feature_count = patches.shape[1]
+    own_normalized = lax.dynamic_slice_in_dim(
+        normalized_rows, lax.axis_index("mp") * feature_count, feature_count, axis=1
+    )
     grad_a_part = lax.dot_general(
-        normalized_wide, adapter_gradient, (((0,), (0,)), ((), ())), precision=lax.Precision.HIGHEST
+        adapter_gradient,
+        own_normalized.astype(jnp.float32),
+        (((0,), (0,)), ((), ())),
+        precision=lax.Precision.HIGHEST,
     )
-    down_gradient = lax.psum(grad_a_part, ("dp", "mp"))
-    grad_b = lax.psum(grad_b_part, "dp")
-    return (embeds_llm, down_gradient * grad_scale, grad_b * grad_scale)
+    down_gradient, grad_b = sum_over_dp(grad_a_part, grad_b_part, rank_count, grad_scale)
+    down_gradient = lax.all_gather(down_gradient, "mp", axis=1, tiled=True).T
+    return (embeds_llm, down_gradient, grad_b)
+
+
+def sum_over_dp(grad_a_part, grad_b_part, rank_count, grad_scale):
+    lanes = 128
+    shares, sizes = [], []
+    for part in (grad_b_part, grad_a_part):
+        share = part.reshape(rank_count, -1)
+        sizes.append(share.shape[1])
+        share = jnp.pad(share, ((0, 0), (0, -share.shape[1] % lanes)))
+        shares.append(share.reshape(rank_count, -1, lanes))
+    cut = shares[0].shape[1]
+    sent = lax.all_to_all(
+        jnp.concatenate(shares, axis=1), "dp", split_axis=0, concat_axis=0, tiled=True
+    )
+    own = jnp.sum(sent, axis=0) * grad_scale
+    whole = lax.all_to_all(
+        jnp.broadcast_to(own[None], (rank_count,) + own.shape),
+        "dp",
+        split_axis=0,
+        concat_axis=0,
+        tiled=True,
+    )
+    grad_b = whole[:, :cut].reshape(rank_count, -1)[:, : sizes[0]].reshape(grad_b_part.shape)
+    grad_a = whole[:, cut:].reshape(rank_count, -1)[:, : sizes[1]].reshape(grad_a_part.shape)
+    return grad_a, grad_b
 
 
 def solution(mesh):

time: 1170 us -> 489 us (0.42)
  waiting for transfers between devices: 1060 us -> 324 us
  blocking collectives: 24.1 us -> 44.5 us
  starting transfers between devices: 38.3 us -> 58.5 us
    psum x2 -> x0, waiting for transfers between devices: 796 us -> none  [the longest x1 464 us: local(): down_gradient = lax.psum(grad_a_part, ('dp', 'mp'))]
    all_to_all x0 -> x2, waiting for transfers between devices: none -> 32.2 us  [the longest x1 32.2 us: sum_over_dp(): lax.all_to_all(jnp.broadcast_to(own[None], (rank_count,) + own.shape), 'd...]
    all_gather x1, waiting for transfers between devices: 116 us -> 88.4 us  [local(): lax.all_gather(first_weight, 'dp', axis=0, tiled=True)]
    all_to_all x1, waiting for transfers between devices: 0.01 us -> 26.7 us  [local(): lax.all_to_all(outgoing, 'dp', split_axis=0, concat_axis=0, tiled=True)]
    reduce_scatter x1, waiting for transfers between devices: 7.71 us -> 29.1 us  [local(): lax.psum_scatter(partial_out.astype(jnp.bfloat16), 'mp', scatter_dimensio...]
    all_to_all x0 -> x2, starting transfers between devices: none -> 20 us  [the longest x1 12.8 us: sum_over_dp(): lax.all_to_all(jnp.concatenate(shares, axis=1), 'dp', split_axis=0, conca...]
    all_gather x0 -> x2, blocking collectives: none -> 20 us  [the longest x1 10.3 us: local(): lax.all_gather(adapter_gradient, 'mp', axis=0)]
    all_to_all x1, waiting for transfers between devices: 0.01 us -> 14.6 us  [local(): lax.all_to_all(language_slot_gradient, 'dp', split_axis=0, concat_axis=0,...]
  transfers between devices with their start and end apart: 7 -> 7, of which waited for: 5 -> 6; matrix products, arithmetic and copies ran while one was open for 3% -> 4% of each run, Pallas kernels for 0% -> 0%
where the time goes in v1:
time: 489 us; the launch traced here: 485 us
  waiting for transfers between devices  324 us (66%)
  starting transfers between devices  58.5 us (12%)
  blocking collectives  44.5 us (9%)
  local copies, waits for them, and re-layouts  26.3 us (5%)
  between operations  14.1 us (3%)
  matrix products  13.3 us (3%)
    all_gather x1, waiting for transfers between devices, local(): lax.all_gather(second_weight, 'dp', axis=1, tiled=True)  131 us
    all_gather x1, waiting for transfers between devices, local(): lax.all_gather(first_weight, 'dp', axis=0, tiled=True)  88.4 us
    all_to_all x1, waiting for transfers between devices, sum_over_dp(): lax.all_to_all(jnp.broadcast_to(own[None], (rank_count,) + own.shape), 'd...  32.2 us
    reduce_scatter x1, waiting for transfers between devices, local(): lax.psum_scatter(partial_out.astype(jnp.bfloat16), 'mp', scatter_dimensio...  29.1 us
    all_to_all x1, waiting for transfers between devices, local(): lax.all_to_all(outgoing, 'dp', split_axis=0, concat_axis=0, tiled=True)  26.7 us
    all_to_all x1, starting transfers between devices, local(): lax.all_to_all(language_slot_gradient, 'dp', split_axis=0, concat_axis=0,...  20.4 us
    all_to_all x1, starting transfers between devices, local(): lax.all_to_all(outgoing, 'dp', split_axis=0, concat_axis=0, tiled=True)  17.8 us
    unnamed x26, local copies, waits for them, and re-layouts  16.2 us
  transfers between devices with their start and end apart: 7, of which 6 were waited for; matrix products, arithmetic and copies ran while one was open for 4% of the time, Pallas kernels for 0%

profile of v1, /device:TPU:1, one launch (start us, length us, event | category | flops | bytes accessed | tf_op | source)
XLA Modules:
  0.0 485.1 jit_solution(5325432834375877393)
XLA Ops:
  7.2 0.0 copy-start
  7.2 0.0 all-gather.7.cloned.1.call-start
  7.3 0.7 all-gather.7.cloned.1.call-update
  8.0 0.0 all-gather.9.cloned.1.call-start
  8.0 0.7 all-gather.9.cloned.1.call-update
  8.7 1.2 copy.29
  9.9 0.0 copy-start.4
  9.9 0.9 all_to_all.25
  10.8 20.4 %all-to-all-start.1 = ((bf16[128,4,320]{2,1,0:T(4,128)(2,1)}), bf16[128,4,320]{2,1,0:T(4,128)(2,1)S(1)}, u32[]{:S(2)}, u32[]{:S(2)}) async-start(bf16[128,4,320]{2,1,0:T(4,128)(2,1)} %all_to_all.25), calls=%async_computation.2 | async-start | bytes 786432 | tf_op jit(solution)/shard_map/all_to_all | solution.py:55
  31.2 0.0 copy-done.8
  31.3 0.1 copy.26
  31.4 0.2 fusion.15
  31.7 12.5 %all_gather.21 = bf16[256,1280]{0,1:T(8,128)(2,1)S(1)} all-gather(bf16[256,320]{0,1:T(8,128)(2,1)S(1)} %copy-done.4), channel_id=1, replica_groups=mesh['dp'=128,'mp'=4] {'mp'}, dimensions={1}, use_global_device_ids=true | all-gather | bytes 819200 | tf_op jit(solution)/shard_map/all_gather | solution.py:59
  44.2 0.2 convert_reduce_fusion
  44.4 0.2 fusion.4
  44.7 0.2 fusion.17
  44.9 0.4 fusion.7
  45.3 0.2 convolution_convert_fusion.3
  45.5 14.6 %all-to-all-done.1 = bf16[128,4,320]{2,1,0:T(4,128)(2,1)S(1)} async-done(((bf16[128,4,320]{2,1,0:T(4,128)(2,1)}), bf16[128,4,320]{2,1,0:T(4,128)(2,1)S(1)}, u32[]{:S(2)}, u32[]{:S(2)}) %all-to-all-start.1) | async-done | bytes 327712 | tf_op jit(solution)/shard_map/all_to_all | solution.py:55
  60.2 0.2 all_to_all.27
  60.4 0.3 convolution_convert_fusion.2
  60.7 12.0 %all_gather.24 = bf16[256,1280]{0,1:T(8,128)(2,1)S(1)} all-gather(bf16[256,320]{0,1:T(8,128)(2,1)S(1)} %convolution_convert_fusion.2), channel_id=1, replica_groups=mesh['dp'=128,'mp'=4] {'mp'}, dimensions={1}, use_global_device_ids=true | all-gather | bytes 819200 | tf_op jit(solution)/shard_map/all_gather | solution.py:84
  72.7 88.4 %all-gather.7.cloned.1.call-done = bf16[128,10,1280]{2,1,0:T(8,128)(2,1)} async-done(((bf16[1,10,1280]{2,1,0:T(8,128)(2,1)}), bf16[128,10,1280]{2,1,0:T(8,128)(2,1)}) %all-gather.7.cloned.1.call-update) | async-done | bytes 3276816 | tf_op jit(solution)/shard_map/all_gather | solution.py:65
  161.0 7.0 %reshape.78 = bf16[1280,1280]{1,0:T(8,128)(2,1)} reshape(bf16[128,10,1280]{2,1,0:T(8,128)(2,1)} %all-gather.7.cloned.1.call-done) | data formatting | bytes 6553600
  168.1 3.0 fusion.23
  171.1 0.4 fusion
  171.4 131.4 %all-gather.9.cloned.1.call-done = bf16[128,10,1280]{2,1,0:T(8,128)(2,1)} async-done(((bf16[1,10,1280]{2,1,0:T(8,128)(2,1)}), bf16[128,10,1280]{2,1,0:T(8,128)(2,1)}) %all-gather.9.cloned.1.call-update) | async-done | bytes 3276816 | tf_op jit(solution)/shard_map/all_gather | solution.py:66
  302.8 7.1 %reshape.80 = bf16[1280,1280]{1,0:T(8,128)(2,1)} reshape(bf16[128,10,1280]{2,1,0:T(8,128)(2,1)} %all-gather.9.cloned.1.call-done) | data formatting | bytes 6553600
  309.9 3.2 fusion.1
  313.1 0.3 fusion.25
  313.4 1.0 fusion.24
  314.5 10.3 %all-gather = f32[1024,64]{0,1:T(8,128)S(1)} all-gather(f32[256,64]{0,1:T(8,128)S(1)} %fusion.25), channel_id=2, replica_groups=mesh['dp'=128,'mp'=4] {'mp'}, dimensions={0}, use_global_device_ids=true | all-gather | bytes 327680 | tf_op jit(solution)/shard_map/all_gather | solution.py:102
  324.8 0.1 reshape.76
  324.9 0.2 reduce_sum.48
  325.1 0.3 fusion.12
  325.4 0.1 reshape.72
  325.4 0.7 pad.4
  326.1 1.8 reshape.73
  327.9 1.9 reshape.71
  329.7 2.0 pad_maximum_fusion
  331.7 12.8 %all-to-all-start.2 = ((f32[128,7,128]{2,1,0:T(8,128)}), f32[128,7,128]{2,1,0:T(8,128)}, u32[]{:S(2)}, u32[]{:S(2)}) async-start(f32[128,7,128]{2,1,0:T(8,128)} %pad_maximum_fusion), calls=%async_computation.3 | async-start | bytes 1048576 | tf_op jit(solution)/shard_map/all_to_all | solution.py:127
  344.6 0.0 copy-start.9
  344.6 0.2 reduce-scatter.2.cloned.1.call-start
  344.8 3.3 convolution_convert_fusion
  348.1 0.0 reduce-scatter.2.cloned.1.call-update
  348.2 29.1 %reduce-scatter.2.cloned.1.call-done = bf16[256,320]{0,1:T(8,128)(2,1)} async-done(((bf16[256,1280]{0,1:T(8,128)(2,1)}), bf16[256,320]{0,1:T(8,128)(2,1)}) %reduce-scatter.2.cloned.1.call-update) | async-done | bytes 163856 | tf_op jit(solution)/shard_map/reduce_scatter | solution.py:76
  377.3 1.3 convolution_convert_fusion.1
  378.6 0.2 copy.28
  378.8 0.9 all_to_all.22
  379.7 0.0 all-to-all-done.2
  379.7 17.8 %all-to-all-start = ((bf16[128,4,320]{2,1,0:T(4,128)(2,1)}), bf16[128,4,320]{2,1,0:T(4,128)(2,1)S(1)}, u32[]{:S(2)}, u32[]{:S(2)}) async-start(bf16[128,4,320]{2,1,0:T(4,128)(2,1)} %all_to_all.22), calls=%async_computation.1 | async-start | bytes 786432 | tf_op jit(solution)/shard_map/all_to_all | solution.py:83
  397.5 1.2 reduce_sum.49
  398.7 26.7 %all-to-all-done = bf16[128,4,320]{2,1,0:T(4,128)(2,1)S(1)} async-done(((bf16[128,4,320]{2,1,0:T(4,128)(2,1)}), bf16[128,4,320]{2,1,0:T(4,128)(2,1)S(1)}, u32[]{:S(2)}, u32[]{:S(2)}) %all-to-all-start) | async-done | bytes 327712 | tf_op jit(solution)/shard_map/all_to_all | solution.py:83
  425.3 0.8 broadcast_in_dim.2
  426.2 7.2 %all-to-all-start.3 = ((f32[128,7,128]{2,1,0:T(8,128)}), f32[128,7,128]{2,1,0:T(8,128)S(1)}, u32[]{:S(2)}, u32[]{:S(2)}) async-start(f32[128,7,128]{2,1,0:T(8,128)} %broadcast_in_dim.2), calls=%async_computation.4 | async-start | bytes 1048576 | tf_op jit(solution)/shard_map/all_to_all | solution.py:131
  433.4 0.2 all_to_all.24
  433.6 0.9 copy.31
  434.5 32.2 %all-to-all-done.3 = f32[128,7,128]{2,1,0:T(8,128)S(1)} async-done(((f32[128,7,128]{2,1,0:T(8,128)}), f32[128,7,128]{2,1,0:T(8,128)S(1)}, u32[]{:S(2)}, u32[]{:S(2)}) %all-to-all-start.3) | async-done | bytes 458784 | tf_op jit(solution)/shard_map/all_to_all | solution.py:131
  466.7 0.1 slice.21
  466.8 0.1 reshape.75
  466.9 9.6 %all-gather.3 = f32[4,320,64]{1,2,0:T(8,128)S(1)} all-gather(f32[1,320,64]{1,2,0:T(8,128)S(1)} %bitcast.52), channel_id=1, replica_groups=mesh['dp'=128,'mp'=4] {'mp'}, dimensions={0}, use_global_device_ids=true | all-gather | bytes 409600 | tf_op jit(solution)/shard_map/all_gather | solution.py:114
  476.5 0.3 copy.30
  476.8 1.0 reshape.82
  477.8 0.8 reshape_reshape.3
  (31 shorter events, 0.2 us)
Async XLA Ops:
  7.2 163.9 %copy-start = (bf16[64,1280]{1,0:T(8,128)(2,1)S(1)}, bf16[64,1280]{1,0:T(8,128)(2,1)}, u32[]{:S(2)}) copy-start(bf16[64,1280]{1,0:T(8,128)(2,1)} %param.18) | copy-start | bytes 491524
  7.2 24.0 %copy-start.6 = (bf16[1280]{0:T(1024)(128)(2,1)S(1)}, bf16[1280]{0:T(1024)(128)(2,1)}, u32[]{:S(2)}) copy-start(bf16[1280]{0:T(1024)(128)(2,1)} %param.13) | copy-start | bytes 7684
  7.2 24.0 %copy-start.7 = (bf16[1280]{0:T(1024)(128)(2,1)S(1)}, bf16[1280]{0:T(1024)(128)(2,1)}, u32[]{:S(2)}) copy-start(bf16[1280]{0:T(1024)(128)(2,1)} %param.14) | copy-start | bytes 7684
  7.2 24.0 %copy-start.8 = (bf16[1280]{0:T(1024)(128)(2,1)S(1)}, bf16[1280]{0:T(1024)(128)(2,1)}, u32[]{:S(2)}) copy-start(bf16[1280]{0:T(1024)(128)(2,1)} %param.16) | copy-start | bytes 7684
  7.2 24.0 %copy-start.5 = (s32[256,1]{0,1:T(1,128)S(1)}, s32[256,1]{0,1:T(1,128)}, u32[]{:S(2)}) copy-start(s32[256,1]{0,1:T(1,128)} %param.12) | copy-start | bytes 3076
  7.2 153.8 %all-gather.7.cloned.1.call-start = ((), (), s32[]{:S(2)}) async-start(), calls=%async_computation.6 | async-start | bytes 5283840 | tf_op jit(solution)/shard_map/all_gather | solution.py:65
  8.0 294.9 %all-gather.9.cloned.1.call-start = ((), (), s32[]{:S(2)}) async-start(), calls=%async_computation.7 | async-start | bytes 5283840 | tf_op jit(solution)/shard_map/all_gather | solution.py:66
  9.9 21.8 %copy-start.4 = (bf16[256,320]{0,1:T(8,128)(2,1)S(1)}, bf16[256,320]{0,1:T(8,128)(2,1)}, u32[]{:S(2)}) copy-start(bf16[256,320]{0,1:T(8,128)(2,1)} %param.11) | copy-start | bytes 491524
  10.8 49.4 %all-to-all-start.1 = ((bf16[128,4,320]{2,1,0:T(4,128)(2,1)}), bf16[128,4,320]{2,1,0:T(4,128)(2,1)S(1)}, u32[]{:S(2)}, u32[]{:S(2)}) async-start(bf16[128,4,320]{2,1,0:T(4,128)(2,1)} %all_to_all.25), calls=%async_computation.2 | async-start | bytes 786432 | tf_op jit(solution)/shard_map/all_to_all | solution.py:55
  44.2 1.0 copy-start.3
  171.4 138.5 %copy-start.2 = (f32[256,1280]{1,0:T(8,128)}, f32[256,1280]{1,0:T(8,128)S(1)}, u32[]{:S(2)}) copy-start(f32[256,1280]{1,0:T(8,128)S(1)} %fusion) | copy-start | bytes 3932164
  326.1 18.7 %copy-start.1 = (bf16[1280,1280]{1,0:T(8,128)(2,1)S(1)}, bf16[1280,1280]{1,0:T(8,128)(2,1)}, u32[]{:S(2)}) copy-start(bf16[1280,1280]{1,0:T(8,128)(2,1)} %reshape.80) | copy-start | bytes 9830404
  331.7 47.9 %all-to-all-start.2 = ((f32[128,7,128]{2,1,0:T(8,128)}), f32[128,7,128]{2,1,0:T(8,128)}, u32[]{:S(2)}, u32[]{:S(2)}) async-start(f32[128,7,128]{2,1,0:T(8,128)} %pad_maximum_fusion), calls=%async_computation.3 | async-start | bytes 1048576 | tf_op jit(solution)/shard_map/all_to_all | solution.py:127
  344.6 3.6 copy-start.9
  344.6 32.7 %reduce-scatter.2.cloned.1.call-start = ((), (), s32[]{:S(2)}) async-start(), calls=%async_computation.5 | async-start | bytes 819200 | tf_op jit(solution)/shard_map/reduce_scatter | solution.py:76
  379.7 45.7 %all-to-all-start = ((bf16[128,4,320]{2,1,0:T(4,128)(2,1)}), bf16[128,4,320]{2,1,0:T(4,128)(2,1)S(1)}, u32[]{:S(2)}, u32[]{:S(2)}) async-start(bf16[128,4,320]{2,1,0:T(4,128)(2,1)} %all_to_all.22), calls=%async_computation.1 | async-start | bytes 786432 | tf_op jit(solution)/shard_map/all_to_all | solution.py:83
  426.2 40.5 %all-to-all-start.3 = ((f32[128,7,128]{2,1,0:T(8,128)}), f32[128,7,128]{2,1,0:T(8,128)S(1)}, u32[]{:S(2)}, u32[]{:S(2)}) async-start(f32[128,7,128]{2,1,0:T(8,128)} %broadcast_in_dim.2), calls=%async_computation.4 | async-start | bytes 1048576 | tf_op jit(solution)/shard_map/all_to_all | solution.py:131
Sparse Core Ops, SparseCore 0:
  11.2 149.8 all-gather.6
  164.2 138.6 all-gather.8
  348.3 28.9 reduce-scatter.1

commit v2 on v1

--- a/solution.py
+++ b/solution.py
@@ -3,7 +3,195 @@
 import jax
 import jax.numpy as jnp
 from jax import lax
+from jax.experimental import pallas as pl
+from jax.experimental.pallas import tpu as pltpu
+
 from jax.sharding import PartitionSpec as P
+
+MESH = pl.DeviceIdType.MESH
+X_CHIPS, Z_CHIPS = 4, 16
+QUAD = 4
+HALF = 8
+
+
+def gather_kernel(
+    pieces_ref, patches_ref, weights_ref, rows_ref,
+    staged, quad_send, quad_recv, y_send, y_recv,
+    ring_send, ring_recv, near_send, near_recv, far_send, far_recv,
+    mate_send, mate_recv,
+):
+    dp, y = lax.axis_index("dp"), lax.axis_index("mp")
+    core = lax.rem(dp, 2)
+    z = lax.rem(dp // 2, Z_CHIPS)
+    x = dp // (2 * Z_CHIPS)
+    turn = 1 - 2 * core
+
+    def dp_of(x_at, z_at, core_at):
+        return (
+            lax.rem(x_at + 2 * X_CHIPS, X_CHIPS) * Z_CHIPS + lax.rem(z_at + 2 * Z_CHIPS, Z_CHIPS)
+        ) * 2 + core_at
+
+    def block_at(x_at, z_at):
+        z_in = lax.rem(z_at + 2 * Z_CHIPS, Z_CHIPS)
+        x_in = lax.rem(x_at + 2 * X_CHIPS, X_CHIPS)
+        return lax.rem(z_in, QUAD) * (X_CHIPS * QUAD) + x_in * QUAD + z_in // QUAD
+
+    quad, lane = z // QUAD, lax.rem(z, QUAD)
+    quad_peers = []
+    for step in range(QUAD):
+        for flip in range(2):
+            if step or flip:
+                other = lax.rem(lane + step, QUAD)
+                quad_peers.append((other, dp_of(x, quad * QUAD + other, (core + flip) % 2)))
+    ring_next = dp_of(x, z + turn, core)
+    ring_last = dp_of(x, z - turn, core)
+    x_next = dp_of(x + turn, z, core)
+    x_last = dp_of(x - turn, z, core)
+    mate = dp_of(x, z, 1 - core)
+
+    barrier = pltpu.get_barrier_semaphore()
+    greeted = [(peer, y) for _, peer in quad_peers]
+    greeted += [(ring_next, y), (ring_last, y), (x_next, y), (x_last, y)]
+    greeted += [(dp, lax.rem(y + step, 4)) for step in range(1, 4)]
+    for peer in greeted:
+        pl.semaphore_signal(barrier, inc=1, device_id=peer, device_id_type=MESH)
+    pl.semaphore_wait(barrier, len(greeted))
+
+    own = lane * 2 + core
+    swaps = []
+    for at, (other, peer) in enumerate(quad_peers):
+        step, flip = (at + 1) // 2, (at + 1) % 2
+        swaps.append(
+            pltpu.make_async_remote_copy(
+                src_ref=pieces_ref.at[other],
+                dst_ref=staged.at[own],
+                send_sem=quad_send.at[at],
+                recv_sem=quad_recv.at[at],
+                device_id=(peer, y),
+                device_id_type=MESH,
+            )
+        )
+        swaps[-1].start()
+    rows_sent = []
+    for step in range(1, 4):
+        rows_sent.append(
+            pltpu.make_async_remote_copy(
+                src_ref=patches_ref,
+                dst_ref=rows_ref.at[y],
+                send_sem=y_send.at[step - 1],
+                recv_sem=y_recv.at[step - 1],
+                device_id=(dp, lax.rem(y + step, 4)),
+                device_id_type=MESH,
+            )
+        )
+        rows_sent[-1].start()
+    staged[own] = pieces_ref[lane]
+    rows_ref[y] = patches_ref[...]
+    for swap in swaps:
+        swap.wait_recv()
+    into = lax.broadcasted_iota(jnp.int32, (80, 128), 0)
+    out_of = lax.broadcasted_iota(jnp.int32, (80, 128), 1)
+    merge = ((into // 10) * 16 + into % 10 == out_of).astype(jnp.bfloat16)
+    mine = block_at(x, z)
+    weights_ref[mine] = jnp.dot(
+        merge, staged[...].reshape(128, 640), preferred_element_type=jnp.float32
+    ).astype(jnp.bfloat16)
+
+    def block_copy(block, sends, recvs, at, peer):
+        return pltpu.make_async_remote_copy(
+            src_ref=weights_ref.at[block],
+            dst_ref=weights_ref.at[block],
+            send_sem=sends.at[at],
+            recv_sem=recvs.at[at],
+            device_id=(peer, y),
+            device_id_type=MESH,
+        )
+
+    sent = []
+
+    def send(block, sends, recvs, at, peer):
+        copy = block_copy(block, sends, recvs, at, peer)
+        copy.start()
+        sent.append(copy)
+
+    def arrived(block, sends, recvs, at):
+        block_copy(block, sends, recvs, at, mate).wait_recv()
+
+    for step in range(HALF + 3):
+        if step <= HALF:
+            if step:
+                arrived(block_at(x, z - turn * step), ring_send, ring_recv, step - 1)
+            first = block_at(x, z - turn * step)
+            if step < HALF:
+                send(first, ring_send, ring_recv, step, ring_next)
+            send(first, near_send, near_recv, 2 * step if step < HALF else 15, x_next)
+            if 0 < step < HALF:
+                send(first, mate_send, mate_recv, step, mate)
+                second = block_at(x, z + turn * step)
+                arrived(second, mate_send, mate_recv, step)
+                send(second, near_send, near_recv, 2 * step - 1, x_next)
+        before = step - 1
+        if 0 <= before <= HALF:
+            at = 2 * before if before < HALF else 15
+            block = block_at(x - turn, z - turn * before)
+            arrived(block, near_send, near_recv, at)
+            if before == 0:
+                @pl.when(core == 0)
+                def _():
+                    block_copy(block, far_send, far_recv, 0, x_next).start()
+            elif before == HALF:
+                @pl.when(core == 1)
+                def _():
+                    block_copy(block, far_send, far_recv, 0, x_next).start()
+            else:
+                send(block, far_send, far_recv, before, x_next)
+            send(block, mate_send, mate_recv, 8 + at, mate)
+            if 0 < before < HALF:
+                block = block_at(x - turn, z + turn * before)
+                arrived(block, near_send, near_recv, 2 * before - 1)
+                send(block, mate_send, mate_recv, 8 + 2 * before - 1, mate)
+        before = step - 2
+        if 0 < before < HALF:
+            block = block_at(x - 2 * turn, z - turn * before)
+            arrived(block, far_send, far_recv, before)
+            send(block, mate_send, mate_recv, 24 + before, mate)
+    block = block_at(x - 2 * turn, z + HALF * core)
+    arrived(block, far_send, far_recv, 0)
+    send(block, mate_send, mate_recv, 24, mate)
+    for at in range(16):
+        arrived(mine, mate_send, mate_recv, 8 + at)
+    for at in range(8):
+        arrived(mine, mate_send, mate_recv, 24 + at)
+    block_copy(mine, far_send, far_recv, 0, x_next).wait_send()
+    for copy in sent + swaps:
+        copy.wait_send()
+    for copy in rows_sent:
+        copy.wait()
+
+
+def gather_all(first_weight, second_weight, patches):
+    rows, columns = first_weight.shape
+    stacked = jnp.stack([first_weight, second_weight.T])
+    stacked = jnp.pad(stacked, ((0, 0), (0, 16 - rows), (0, 0)))
+    pieces = stacked.reshape(2, 16, 2, columns // 2).transpose(0, 2, 1, 3).reshape(4, 16, 640)
+    whole = pl.BlockSpec(memory_space=pltpu.VMEM)
+    semaphores = [7, 7, 3, 3, 8, 8, 16, 16, 8, 8, 32, 32]
+    weights, rows = pl.pallas_call(
+        gather_kernel,
+        out_shape=(
+            jax.ShapeDtypeStruct((64, 80, 640), jnp.bfloat16),
+            jax.ShapeDtypeStruct((4,) + patches.shape, jnp.bfloat16),
+        ),
+        in_specs=[whole, whole],
+        out_specs=(whole, whole),
+        scratch_shapes=[pltpu.VMEM((8, 16, 640), jnp.bfloat16)]
+        + [pltpu.SemaphoreType.DMA((count,)) for count in semaphores],
+        compiler_params=pltpu.CompilerParams(
+            collective_id=0, has_side_effects=True, vmem_limit_bytes=32 * 1024 * 1024
+        ),
+        name="gather",
+    )(pieces, patches)
+    return weights.reshape(2, 2, 1280, 640), rows
 
 
 def quick_gelu(values):
@@ -56,23 +244,32 @@
     grad_local = lax.dot_general(
         placing, returned, (((0,), (0,)), ((), ())), preferred_element_type=jnp.float32
     ).astype(jnp.bfloat16)
-    whole_rows = lax.all_gather(patches, "mp", axis=1, tiled=True)
+    projections, rows_by_rank = gather_all(first_weight, second_weight, patches)
+    whole_rows = jnp.concatenate(list(rows_by_rank), axis=1)
     normalized_rows = normalize(whole_rows, gain, shift)
     adapter_latent = jnp.dot(
         normalized_rows, adapter_down, preferred_element_type=jnp.float32
     ).astype(jnp.bfloat16)
-    first_full, second_full = (
-        lax.all_gather(first_weight, "dp", axis=0, tiled=True),
-        lax.all_gather(second_weight, "dp", axis=1, tiled=True),
-    )
-    pre_main = jnp.dot(normalized_rows, first_full, preferred_element_type=jnp.float32)
+    pre_main = jnp.concatenate(
+        [
+            jnp.dot(normalized_rows, half, preferred_element_type=jnp.float32)
+            for half in projections[0]
+        ],
+        axis=1,
+    )
     preactivation = (
         pre_main
         + jnp.dot(adapter_latent, adapter_up, preferred_element_type=jnp.float32)
         + first_bias.astype(jnp.float32)
     )
     activated = quick_gelu(preactivation).astype(jnp.bfloat16)
-    partial_out = jnp.dot(activated, second_full, preferred_element_type=jnp.float32)
+    hidden_halves = jnp.split(activated, 2, axis=1)
+    partial_out = sum(
+        lax.dot_general(
+            part, half, (((1,), (1,)), ((), ())), preferred_element_type=jnp.float32
+        )
+        for part, half in zip(hidden_halves, projections[1])
+    )
     branch_out = lax.psum_scatter(
         partial_out.astype(jnp.bfloat16), "mp", scatter_dimension=1, tiled=True
     ).astype(jnp.float32)
@@ -82,8 +279,12 @@
     outgoing = jnp.dot(placing, embeds, preferred_element_type=jnp.float32).astype(jnp.bfloat16)
     embeds_llm = lax.all_to_all(outgoing, "dp", split_axis=0, concat_axis=0, tiled=True)
     whole_grad = lax.all_gather(grad_local, "mp", axis=1, tiled=True)
-    grad_act = lax.dot_general(
-        whole_grad, second_full, (((1,), (1,)), ((), ())), preferred_element_type=jnp.float32
+    grad_act = jnp.concatenate(
+        [
+            jnp.dot(whole_grad, half, preferred_element_type=jnp.float32)
+            for half in projections[1]
+        ],
+        axis=1,
     )
     preactivation_gradient = (grad_act * gelu_slope(preactivation)).astype(jnp.bfloat16)
     adapter_gradient = lax.dot_general(

time: 489 us -> 308 us (0.63)
  waiting for transfers between devices: 324 us -> 88.3 us
  Pallas kernels: 0 us -> 65.2 us
  blocking collectives: 44.5 us -> 31.5 us
    all_gather x2 -> x0, waiting for transfers between devices: 220 us -> none  [the longest x1 131 us: local(): lax.all_gather(second_weight, 'dp', axis=1, tiled=True)]
    pallas_call x0 -> x1, Pallas kernels: none -> 65.2 us  [gather_all(): pl.pallas_call(gather_kernel, out_shape=(jax.ShapeDtypeStruct((64, 80, 64...]
    all_to_all x1, waiting for transfers between devices: 14.6 us -> 0.01 us  [local(): lax.all_to_all(language_slot_gradient, 'dp', split_axis=0, concat_axis=0,...]
    all_gather x1 -> x0, blocking collectives: 12.5 us -> none  [local(): whole_rows = lax.all_gather(patches, 'mp', axis=1, tiled=True)]
    unnamed x26 -> x39, local copies, waits for them, and re-layouts: 16.2 us -> 6.17 us
  transfers between devices with their start and end apart: 7 -> 5, of which waited for: 6 -> 3; matrix products, arithmetic and copies ran while one was open for 4% -> 5% of each run, Pallas kernels for 0% -> 21%
where the time goes in v2:
time: 308 us; the launch traced here: 304 us
  waiting for transfers between devices  88.3 us (29%)
  Pallas kernels  65.2 us (21%)
  starting transfers between devices  58.2 us (19%)
  blocking collectives  31.5 us (10%)
  local copies, waits for them, and re-layouts  25.1 us (8%)
  matrix products  14.9 us (5%)
  between operations  14.5 us (5%)
  other arithmetic  6.25 us (2%)
    pallas_call x1, Pallas kernels, gather_all(): pl.pallas_call(gather_kernel, out_shape=(jax.ShapeDtypeStruct((64, 80, 64...  65.2 us
    all_to_all x1, waiting for transfers between devices, sum_over_dp(): lax.all_to_all(jnp.broadcast_to(own[None], (rank_count,) + own.shape), 'd...  32.2 us
    reduce_scatter x1, waiting for transfers between devices, local(): lax.psum_scatter(partial_out.astype(jnp.bfloat16), 'mp', scatter_dimensio...  29.4 us
    all_to_all x1, waiting for transfers between devices, local(): lax.all_to_all(outgoing, 'dp', split_axis=0, concat_axis=0, tiled=True)  26.7 us
    all_to_all x1, starting transfers between devices, local(): lax.all_to_all(language_slot_gradient, 'dp', split_axis=0, concat_axis=0,...  20.8 us
    all_to_all x1, starting transfers between devices, local(): lax.all_to_all(outgoing, 'dp', split_axis=0, concat_axis=0, tiled=True)  17.8 us
    all_to_all x1, starting transfers between devices, sum_over_dp(): lax.all_to_all(jnp.concatenate(shares, axis=1), 'dp', split_axis=0, conca...  12.4 us
    all_gather x1, blocking collectives, local(): whole_grad = lax.all_gather(grad_local, 'mp', axis=1, tiled=True)  11.7 us
  transfers between devices with their start and end apart: 5, of which 3 were waited for; matrix products, arithmetic and copies ran while one was open for 5% of the time, Pallas kernels for 21%

profile of v2, /device:TPU:1, one launch (start us, length us, event | category | flops | bytes accessed | tf_op | source)
XLA Modules:
  0.0 304.1 jit_solution(13310296270335690239)
XLA Ops:
  7.2 0.0 copy-start
  7.2 1.2 copy.33
  8.5 0.9 all_to_all.25
  9.3 20.8 %all-to-all-start.1 = ((bf16[128,4,320]{2,1,0:T(4,128)(2,1)}), bf16[128,4,320]{2,1,0:T(4,128)(2,1)}, u32[]{:S(2)}, u32[]{:S(2)}) async-start(bf16[128,4,320]{2,1,0:T(4,128)(2,1)} %all_to_all.25), calls=%async_computation.2 | async-start | bytes 786432 | tf_op jit(solution)/shard_map/all_to_all | solution.py:243
  30.2 0.2 copy.31.patches_ref
  30.4 65.2 %gather.1 = (bf16[64,80,640]{2,1,0:T(8,128)(2,1)S(1)}, bf16[4,256,320]{2,1,0:T(8,128)(2,1)S(1)}) custom-call(bf16[4,16,640]{2,1,0:T(8,128)(2,1)S(1)} %bitcast.65, bf16[256,320]{1,0:T(8,128)(2,1)S(1)} %copy.31.patches_ref), custom_call_target="tpu_custom_call" | custom-call | tf_op jit(solution)/shard_map/gather/pallas_call | solution.py:179
  95.6 2.7 copy-done.1
  98.4 0.1 slice_bitcast_fusion
  98.5 0.0 copy-start.12
  98.5 0.5 concatenate.16
  99.0 0.2 convert_reduce_fusion
  99.1 0.3 fusion.4
  99.5 0.0 copy-start.9
  99.5 0.1 copy.29
  99.7 0.2 fusion.19
  100.0 0.2 fusion.21
  100.1 0.3 fusion.7
  100.5 0.3 convolution_convert_fusion.2
  100.8 0.5 copy-done.2
  101.3 3.5 %fusion.26 = (bf16[16,80,640]{2,1,0:T(8,128)(2,1)S(1)}, bf16[16,80,640]{2,1,0:T(8,128)(2,1)S(1)}, bf16[16,80,640]{2,1,0:T(8,128)(2,1)S(1)}, bf16[16,80,640]{2,1,0:T(8,128)(2,1)S(1)}) fusion(bf16[64,80,640]{2,1,0:T(8,128)(2,1)} %copy-done.1), kind=kLoop, calls=%fused_computation.55 | loop fusion | bytes 13107200 | tf_op jit(solution)/shard_map/unstack | solution.py:271
  104.9 1.5 fusion.28
  106.4 1.5 fusion.29
  108.0 1.9 all_to_all.27
  109.9 1.3 convolution_convert_fusion.1
  111.2 11.7 %all_gather.12 = bf16[256,1280]{0,1:T(8,128)(2,1)S(1)} all-gather(bf16[256,320]{0,1:T(8,128)(2,1)S(1)} %convolution_convert_fusion.1), channel_id=1, replica_groups=mesh['dp'=128,'mp'=4] {'mp'}, dimensions={1}, use_global_device_ids=true | all-gather | bytes 819200 | tf_op jit(solution)/shard_map/all_gather | solution.py:281
  123.0 0.7 fusion.30
  123.7 0.7 fusion.31
  124.4 0.3 copy-done.5
  124.8 0.2 copy-done.6
  125.0 1.7 fusion.8
  126.7 1.0 fusion.32
  127.6 0.3 fusion.33
  127.9 1.9 reshape.89
  129.9 10.1 %all-gather = f32[1024,64]{0,1:T(8,128)} all-gather(f32[256,64]{0,1:T(8,128)S(1)} %fusion.33), channel_id=2, replica_groups=mesh['dp'=128,'mp'=4] {'mp'}, dimensions={0}, use_global_device_ids=true | all-gather | bytes 327680 | tf_op jit(solution)/shard_map/all_gather | solution.py:303
  140.0 1.8 reshape.94
  141.7 1.7 reduce_sum.48
  143.5 1.3 fusion.14
  144.8 0.7 reshape.90
  145.5 1.6 pad.9
  147.1 1.6 reshape.91
  148.7 2.0 pad_maximum_fusion
  150.7 12.4 %all-to-all-start.2 = ((f32[128,7,128]{2,1,0:T(8,128)}), f32[128,7,128]{2,1,0:T(8,128)}, u32[]{:S(2)}, u32[]{:S(2)}) async-start(f32[128,7,128]{2,1,0:T(8,128)} %pad_maximum_fusion), calls=%async_computation.3 | async-start | bytes 1048576 | tf_op jit(solution)/shard_map/all_to_all | solution.py:328
  163.2 0.0 reduce-scatter.2.cloned.1.call-start
  163.2 1.8 fusion.10
  165.0 1.6 fusion.1
  166.6 0.0 reduce-scatter.2.cloned.1.call-update
  166.7 29.4 %reduce-scatter.2.cloned.1.call-done = bf16[256,320]{0,1:T(8,128)(2,1)} async-done(((bf16[256,1280]{0,1:T(8,128)(2,1)}), bf16[256,320]{0,1:T(8,128)(2,1)}) %reduce-scatter.2.cloned.1.call-update) | async-done | bytes 163856 | tf_op jit(solution)/shard_map/reduce_scatter | solution.py:273
  196.1 1.2 convolution_convert_fusion
  197.3 0.2 copy.32
  197.5 0.9 all_to_all.22
  198.4 17.8 %all-to-all-start = ((bf16[128,4,320]{2,1,0:T(4,128)(2,1)}), bf16[128,4,320]{2,1,0:T(4,128)(2,1)S(1)}, u32[]{:S(2)}, u32[]{:S(2)}) async-start(bf16[128,4,320]{2,1,0:T(4,128)(2,1)} %all_to_all.22), calls=%async_computation.1 | async-start | bytes 786432 | tf_op jit(solution)/shard_map/all_to_all | solution.py:280
  216.2 1.2 reduce_sum.49
  217.3 26.7 %all-to-all-done = bf16[128,4,320]{2,1,0:T(4,128)(2,1)S(1)} async-done(((bf16[128,4,320]{2,1,0:T(4,128)(2,1)}), bf16[128,4,320]{2,1,0:T(4,128)(2,1)S(1)}, u32[]{:S(2)}, u32[]{:S(2)}) %all-to-all-start) | async-done | bytes 327712 | tf_op jit(solution)/shard_map/all_to_all | solution.py:280
  244.0 0.8 broadcast_in_dim.2
  244.8 7.2 %all-to-all-start.3 = ((f32[128,7,128]{2,1,0:T(8,128)}), f32[128,7,128]{2,1,0:T(8,128)S(1)}, u32[]{:S(2)}, u32[]{:S(2)}) async-start(f32[128,7,128]{2,1,0:T(8,128)} %broadcast_in_dim.2), calls=%async_computation.4 | async-start | bytes 1048576 | tf_op jit(solution)/shard_map/all_to_all | solution.py:332
  252.0 0.2 all_to_all.24
  252.2 0.9 copy.35
  253.1 32.2 %all-to-all-done.3 = f32[128,7,128]{2,1,0:T(8,128)S(1)} async-done(((f32[128,7,128]{2,1,0:T(8,128)}), f32[128,7,128]{2,1,0:T(8,128)S(1)}, u32[]{:S(2)}, u32[]{:S(2)}) %all-to-all-start.3) | async-done | bytes 458784 | tf_op jit(solution)/shard_map/all_to_all | solution.py:332
  285.4 0.1 slice.44
  285.5 0.1 reshape.93
  285.5 9.6 %all-gather.1 = f32[4,320,64]{1,2,0:T(8,128)S(1)} all-gather(f32[1,320,64]{1,2,0:T(8,128)S(1)} %bitcast.77), channel_id=1, replica_groups=mesh['dp'=128,'mp'=4] {'mp'}, dimensions={0}, use_global_device_ids=true | all-gather | bytes 409600 | tf_op jit(solution)/shard_map/all_gather | solution.py:315
  295.2 0.3 copy.34
  295.4 1.0 reshape.96
  296.4 0.8 reshape_reshape.3
  (47 shorter events, 0.2 us)
Async XLA Ops:
  7.2 117.3 %copy-start = (bf16[64,1280]{1,0:T(8,128)(2,1)S(1)}, bf16[64,1280]{1,0:T(8,128)(2,1)}, u32[]{:S(2)}) copy-start(bf16[64,1280]{1,0:T(8,128)(2,1)} %param.18) | copy-start | bytes 491524
  7.2 22.9 %copy-start.11 = (bf16[10,1280]{1,0:T(8,128)(2,1)S(1)}, bf16[10,1280]{1,0:T(8,128)(2,1)}, u32[]{:S(2)}) copy-start(bf16[10,1280]{1,0:T(8,128)(2,1)} %param.15) | copy-start | bytes 76804
  7.2 22.9 %copy-start.10 = (bf16[1280,10]{0,1:T(8,128)(2,1)S(1)}, bf16[1280,10]{0,1:T(8,128)(2,1)}, u32[]{:S(2)}) copy-start(bf16[1280,10]{0,1:T(8,128)(2,1)} %param.19) | copy-start | bytes 76804
  7.2 23.0 %copy-start.7 = (bf16[256,320]{0,1:T(8,128)(2,1)S(1)}, bf16[256,320]{0,1:T(8,128)(2,1)}, u32[]{:S(2)}) copy-start(bf16[256,320]{0,1:T(8,128)(2,1)} %param.11) | copy-start | bytes 491524
  9.3 98.6 %all-to-all-start.1 = ((bf16[128,4,320]{2,1,0:T(4,128)(2,1)}), bf16[128,4,320]{2,1,0:T(4,128)(2,1)}, u32[]{:S(2)}, u32[]{:S(2)}) async-start(bf16[128,4,320]{2,1,0:T(4,128)(2,1)} %all_to_all.25), calls=%async_computation.2 | async-start | bytes 786432 | tf_op jit(solution)/shard_map/all_to_all | solution.py:243
  95.6 2.7 copy-start.1
  98.4 1.0 copy-start.13
  98.5 1.1 copy-start.14
  98.5 1.1 copy-start.12
  99.5 1.1 copy-start.15
  99.5 1.1 copy-start.9
  100.5 0.9 copy-start.2
  101.3 3.5 %copy-start.3 = (bf16[256,1280]{1,0:T(8,128)(2,1)S(1)}, bf16[256,1280]{1,0:T(8,128)(2,1)}, u32[]{:S(2)}) copy-start(bf16[256,1280]{1,0:T(8,128)(2,1)} %copy-done.2) | copy-start | bytes 1966084
  123.7 1.1 copy-start.5
  123.7 1.3 copy-start.6
  150.7 47.7 %all-to-all-start.2 = ((f32[128,7,128]{2,1,0:T(8,128)}), f32[128,7,128]{2,1,0:T(8,128)}, u32[]{:S(2)}, u32[]{:S(2)}) async-start(f32[128,7,128]{2,1,0:T(8,128)} %pad_maximum_fusion), calls=%async_computation.3 | async-start | bytes 1048576 | tf_op jit(solution)/shard_map/all_to_all | solution.py:328
  163.2 32.9 %reduce-scatter.2.cloned.1.call-start = ((), (), s32[]{:S(2)}) async-start(), calls=%async_computation.5 | async-start | bytes 819200 | tf_op jit(solution)/shard_map/reduce_scatter | solution.py:273
  163.2 1.8 copy-start.4
  165.0 1.6 copy-start.16
  165.0 31.1 %copy-start.8 = (bf16[256,320]{0,1:T(8,128)(2,1)S(1)}, bf16[256,320]{0,1:T(8,128)(2,1)}, u32[]{:S(2)}) copy-start(bf16[256,320]{0,1:T(8,128)(2,1)} %param.11) | copy-start | bytes 491524
  198.4 45.6 %all-to-all-start = ((bf16[128,4,320]{2,1,0:T(4,128)(2,1)}), bf16[128,4,320]{2,1,0:T(4,128)(2,1)S(1)}, u32[]{:S(2)}, u32[]{:S(2)}) async-start(bf16[128,4,320]{2,1,0:T(4,128)(2,1)} %all_to_all.22), calls=%async_computation.1 | async-start | bytes 786432 | tf_op jit(solution)/shard_map/all_to_all | solution.py:280
  244.8 40.5 %all-to-all-start.3 = ((f32[128,7,128]{2,1,0:T(8,128)}), f32[128,7,128]{2,1,0:T(8,128)S(1)}, u32[]{:S(2)}, u32[]{:S(2)}) async-start(f32[128,7,128]{2,1,0:T(8,128)} %broadcast_in_dim.2), calls=%async_computation.4 | async-start | bytes 1048576 | tf_op jit(solution)/shard_map/all_to_all | solution.py:332
Sparse Core Ops, SparseCore 0:
  166.8 29.2 reduce-scatter.1

commit v3 on v0

v3 whole, which is shorter than its diff:
```python
import math

import jax
import jax.numpy as jnp
from jax import lax
from jax.experimental import pallas as pl
from jax.experimental.pallas import tpu as pltpu
from jax.sharding import PartitionSpec as P

MESH = pl.DeviceIdType.MESH
X_CHIPS, Z_CHIPS, MP = 4, 16, 4
QUAD, HALF, OCT = 4, 8, 8
TILES, SUM_TILES = 16, 13
GRAD_B_TILES = 10


def one_hot(places, count):
    columns = lax.broadcasted_iota(jnp.int32, (places.shape[0], count), 1)
    return (columns == places).astype(jnp.bfloat16)


def f32_dot(a, b):
    return jnp.dot(a, b, preferred_element_type=jnp.float32)


def f32_dot_t(a, b):
    return lax.dot_general(a, b, (((1,), (1,)), ((), ())), preferred_element_type=jnp.float32)


def block_kernel(
    pieces_ref, patches_ref, slots_ref, place_row_ref, place_col_ref, gain_ref, shift_ref,
    first_bias_ref, down_ref, down_t_ref, up_ref, second_bias_ref,
    embeds_ref, grad_a_ref, grad_b_ref,
    weights, staged, rows, normed, grads, act, slope, partial, got_partial,
    in_a, in_b, in_c, in_e, out_a, out_b, out_c, out_e,
    lora, parts, got_parts, reduced, got_tiles, total, whole_b, rank_a, whole_a,
    quad_send, quad_recv, ring_send, ring_recv, near_send, near_recv, far_send, far_recv,
    mate_send, mate_recv, y_send, y_recv, z_send, z_recv, oct_send, oct_recv,
):
    dp, y = lax.axis_index("dp"), lax.axis_index("mp")
    core = lax.rem(dp, 2)
    z = lax.rem(dp // 2, Z_CHIPS)
    x = dp // (2 * Z_CHIPS)
    turn = 1 - 2 * core
    own_oct = x * 2 + core

    def dp_of(x_at, z_at, core_at):
        return (
            lax.rem(x_at + 2 * X_CHIPS, X_CHIPS) * Z_CHIPS + lax.rem(z_at + 2 * Z_CHIPS, Z_CHIPS)
        ) * 2 + core_at

    def block_at(x_at, z_at):
        z_in = lax.rem(z_at + 2 * Z_CHIPS, Z_CHIPS)
        x_in = lax.rem(x_at + 2 * X_CHIPS, X_CHIPS)
        return lax.rem(z_in, QUAD) * (X_CHIPS * QUAD) + x_in * QUAD + z_in // QUAD

    quad, lane = z // QUAD, lax.rem(z, QUAD)
    quad_peers = []
    for step in range(QUAD):
        for flip in range(2):
            if step or flip:
                other = lax.rem(lane + step, QUAD)
                quad_peers.append((other, dp_of(x, quad * QUAD + other, lax.rem(core + flip, 2))))
    ring_next = dp_of(x, z + turn, core)
    x_next = dp_of(x + turn, z, core)
    mate = dp_of(x, z, 1 - core)
    z_peers = [lax.rem(z + step, Z_CHIPS) for step in range(1, Z_CHIPS)]
    y_peers = [lax.rem(y + step, MP) for step in range(1, MP)]
    oct_peers = []
    for step in range(1, OCT):
        x_at, core_at = lax.rem(x + step // 2, X_CHIPS), lax.rem(core + step % 2, 2)
        oct_peers.append((x_at * 2 + core_at, dp_of(x_at, z, core_at)))

    barrier = pltpu.get_barrier_semaphore()
    greeted = [(peer, y) for _, peer in quad_peers]
    greeted += [(dp_of(x, z_at, core), y) for z_at in z_peers]
    greeted += [(peer, y) for _, peer in oct_peers]
    greeted += [(dp, y_at) for y_at in y_peers]
    for peer in greeted:
        pl.semaphore_signal(barrier, inc=1, device_id=peer, device_id_type=MESH)
    pl.semaphore_wait(barrier, len(greeted))

    sent = []

    def send(source, target, send_sem, recv_sem, peer, peer_y=None):
        copy = pltpu.make_async_remote_copy(
            src_ref=source,
            dst_ref=target,
            send_sem=send_sem,
            recv_sem=recv_sem,
            device_id=(peer, y if peer_y is None else peer_y),
            device_id_type=MESH,
        )
        copy.start()
        sent.append(copy)
        return copy

    def wait_all(copies):
        for copy in copies:
            copy.wait_recv()

    def to_y(buffer, phase):
        return [
            send(buffer.at[y], buffer.at[y], y_send.at[3 * phase + at], y_recv.at[3 * phase + at],
                 dp, y_at)
            for at, y_at in enumerate(y_peers)
        ]

    def to_z(source, target, phase):
        first = 15 * phase
        return [
            send(source.at[z_at], target.at[z], z_send.at[first + at], z_recv.at[first + at],
                 dp_of(x, z_at, core))
            for at, z_at in enumerate(z_peers)
        ]

    def to_oct(source_of, target, phase):
        first = 7 * phase
        return [
            send(source_of(at_oct), target, oct_send.at[first + at], oct_recv.at[first + at], peer)
            for at, (at_oct, peer) in enumerate(oct_peers)
        ]

    def block_copy(block, sends, recvs, at, peer):
        return pltpu.make_async_remote_copy(
            src_ref=weights.at[block],
            dst_ref=weights.at[block],
            send_sem=sends.at[at],
            recv_sem=recvs.at[at],
            device_id=(peer, y),
            device_id_type=MESH,
        )

    def send_block(block, sends, recvs, at, peer):
        copy = block_copy(block, sends, recvs, at, peer)
        copy.start()
        sent.append(copy)

    def arrived(block, sends, recvs, at):
        block_copy(block, sends, recvs, at, mate).wait_recv()

    def row_places(count):
        return lax.broadcasted_iota(jnp.int32, (count, 1), 0)

    def regroup_for_oct(received):
        n = row_places(512)
        place = (n // 4 % 16) * 32 + (n // 64) * 4 + n % 4
        return f32_dot(one_hot(place, 512), received[...].reshape(512, 320)).astype(
            jnp.bfloat16
        ).reshape(OCT, 64, 320)

    own = lane * 2 + core
    swaps = [
        send(pieces_ref.at[other], staged.at[own], quad_send.at[at], quad_recv.at[at], peer)
        for at, (other, peer) in enumerate(quad_peers)
    ]
    rows[y] = patches_ref[...]
    row_copies = to_y(rows, 0)
    staged[own] = pieces_ref[lane]

    n = row_places(512)
    place = (n // 8 % 4) * 128 + (n // 32) * 8 + n % 8
    in_a[...] = f32_dot(one_hot(place, 512), slots_ref[...]).astype(jnp.bfloat16).reshape(
        Z_CHIPS, 32, 320
    )
    in_b[z] = in_a[z]
    slot_copies = to_z(in_a, in_b, 0)

    wait_all(swaps)
    n = row_places(80)
    mine = block_at(x, z)
    weights[mine] = f32_dot(
        one_hot(n // 10 * 16 + n % 10, 128), staged[...].reshape(128, 640)
    ).astype(jnp.bfloat16)

    latents = []

    def norm_rows():
        wait_all(row_copies)
        floats = [rows[j].astype(jnp.float32) for j in range(MP)]
        mean = sum(jnp.sum(f, axis=-1, keepdims=True) for f in floats) * (1.0 / 1280)
        centred = [f - mean for f in floats]
        var = sum(jnp.sum(c * c, axis=-1, keepdims=True) for c in centred) * (1.0 / 1280)
        scale = lax.rsqrt(var + 1e-06)
        for j in range(MP):
            normed[j] = (centred[j] * scale * gain_ref[j] + shift_ref[j]).astype(jnp.bfloat16)
        latents.append(
            sum(f32_dot(normed[j], down_ref[j]) for j in range(MP)).astype(jnp.bfloat16)
        )
        latents.append(
            sum(f32_dot_t(down_t_ref[j], normed[j]) for j in range(MP)).astype(jnp.bfloat16)
        )

    slot_steps = []

    def slots_to_oct():
        wait_all(slot_copies)
        in_c[...] = regroup_for_oct(in_b)
        in_e[own_oct] = in_c[own_oct]
        slot_steps.append(to_oct(lambda o: in_c.at[o], in_e.at[own_oct], 0))

    def pick_grads():
        wait_all(slot_steps[0])
        grads[y] = f32_dot(
            one_hot(place_col_ref[...], 512), in_e[...].reshape(512, 320)
        ).astype(jnp.bfloat16)
        slot_steps.append(to_y(grads, 1))

    between = {2: norm_rows, 6: slots_to_oct, 9: pick_grads}

    for step in range(HALF + 3):
        if step <= HALF:
            if step:
                arrived(block_at(x, z - turn * step), ring_send, ring_recv, step - 1)
            first = block_at(x, z - turn * step)
            if step < HALF:
                send_block(first, ring_send, ring_recv, step, ring_next)
            send_block(first, near_send, near_recv, 2 * step if step < HALF else 15, x_next)
            if 0 < step < HALF:
                send_block(first, mate_send, mate_recv, step, mate)
                second = block_at(x, z + turn * step)
                arrived(second, mate_send, mate_recv, step)
                send_block(second, near_send, near_recv, 2 * step - 1, x_next)
        before = step - 1
        if 0 <= before <= HALF:
            at = 2 * before if before < HALF else 15
            block = block_at(x - turn, z - turn * before)
            arrived(block, near_send, near_recv, at)
            if before == 0:
                @pl.when(core == 0)
                def _():
                    block_copy(block, far_send, far_recv, 0, x_next).start()
            elif before == HALF:
                @pl.when(core == 1)
                def _():
                    block_copy(block, far_send, far_recv, 0, x_next).start()
            else:
                send_block(block, far_send, far_recv, before, x_next)
            send_block(block, mate_send, mate_recv, 8 + at, mate)
            if 0 < before < HALF:
                block = block_at(x - turn, z + turn * before)
                arrived(block, near_send, near_recv, 2 * before - 1)
                send_block(block, mate_send, mate_recv, 8 + 2 * before - 1, mate)
        before = step - 2
        if 0 < before < HALF:
            block = block_at(x - 2 * turn, z - turn * before)
            arrived(block, far_send, far_recv, before)
            send_block(block, mate_send, mate_recv, 24 + before, mate)
        if step in between:
            between[step]()
    block = block_at(x - 2 * turn, z + HALF * core)
    arrived(block, far_send, far_recv, 0)
    send_block(block, mate_send, mate_recv, 24, mate)
    for at in range(8, 32):
        arrived(mine, mate_send, mate_recv, at)

    latent, latent_t = latents

    def first_block(j, half):
        return weights[half * 16 + j * 4:half * 16 + j * 4 + 4].reshape(320, 640)

    def second_block(j, half):
        return weights[pl.ds((2 + half) * 16 + j * 4, 4)].reshape(320, 640)

    for half in range(2):
        pre = sum(f32_dot(normed[j], first_block(j, half)) for j in range(MP))
        pre = pre + f32_dot(latent, up_ref[half]) + first_bias_ref[half]
        sigma = jax.nn.sigmoid(1.702 * pre)
        act[half] = (pre * sigma).astype(jnp.bfloat16)
        slope[half] = sigma + 1.702 * pre * sigma * (1.0 - sigma)
    partial_copies = []
    for step in (1, 2, 3, 0):
        y_at = lax.rem(y + step, MP)
        partial[step] = sum(
            f32_dot_t(act[half], second_block(y_at, half)) for half in range(2)
        ).astype(jnp.bfloat16)
        if step:
            partial_copies.append(
                send(partial.at[step], got_partial.at[step - 1], y_send.at[5 + step],
                     y_recv.at[5 + step], dp, y_at)
            )

    wait_all(slot_steps[1])
    lora_t = jnp.zeros((64, 256), jnp.float32)
    for half in range(2):
        grad_act = sum(f32_dot(grads[j], second_block(j, half)) for j in range(MP))
        grad_pre = (grad_act * slope[half]).astype(jnp.bfloat16)
        lora_t = lora_t + f32_dot_t(up_ref[half], grad_pre)
        grad_b = f32_dot(latent_t, grad_pre)
        for o in range(OCT):
            for tile in range(5):
                parts[o, half * 5 + tile] = grad_b[8 * o:8 * o + 8, 128 * tile:128 * tile + 128]
    lora[y] = lora_t
    lora_copies = to_y(lora, 3)

    wait_all(partial_copies)
    branch = partial[0].astype(jnp.float32)
    for at in range(3):
        branch = branch + got_partial[at].astype(jnp.float32)
    embeds = (patches_ref[...].astype(jnp.float32) + branch + second_bias_ref[...]).astype(
        jnp.bfloat16
    )
    placing = (row_places(512) == place_row_ref[...]).astype(jnp.bfloat16)
    out_a[...] = f32_dot(placing, embeds).astype(jnp.bfloat16).reshape(Z_CHIPS, 32, 320)
    out_b[z] = out_a[z]
    out_copies = to_z(out_a, out_b, 1)

    wait_all(lora_copies)
    rest = lora[0] + lora[1] + lora[2] + lora[3]
    grad_a = jnp.zeros((64, 320), jnp.float32)
    own_normed = normed[y]
    for _ in range(3):
        top = rest.astype(jnp.bfloat16)
        rest = rest - top.astype(jnp.float32)
        grad_a = grad_a + f32_dot(top, own_normed)
    for o in range(OCT):
        strip = grad_a[8 * o:8 * o + 8]
        parts[o, 10] = strip[:, 0:128]
        parts[o, 11] = strip[:, 128:256]
        parts[o, 12] = jnp.concatenate([strip[:, 256:320], jnp.zeros((8, 64), jnp.float32)], 1)
    got_parts[own_oct] = parts[own_oct]
    part_copies = to_oct(lambda o: parts.at[o], got_parts.at[own_oct], 1)

    wait_all(part_copies)
    reduced[0:SUM_TILES] = jnp.sum(got_parts[...], axis=0)
    reduced[SUM_TILES:TILES] = jnp.zeros((TILES - SUM_TILES, 8, 128), jnp.float32)
    got_tiles[z] = reduced[z]
    tile_copies = to_z(reduced, got_tiles, 2)

    wait_all(out_copies)
    out_c[...] = regroup_for_oct(out_b)
    out_e[own_oct] = out_c[own_oct]
    oct_copies = to_oct(lambda o: out_c.at[o], out_e.at[own_oct], 2)

    wait_all(tile_copies)
    total[z] = jnp.sum(got_tiles[...], axis=0) * (1.0 / math.sqrt(32768))
    total_copies = [
        send(total.at[z], total.at[z], z_send.at[45 + at], z_recv.at[45 + at],
             dp_of(x, z_at, core))
        for at, z_at in enumerate(z_peers)
    ]

    wait_all(total_copies)
    rank_a[y] = total[GRAD_B_TILES:SUM_TILES]
    rank_copies = to_y(rank_a, 4)
    whole_b[own_oct] = total[0:GRAD_B_TILES]
    whole_b_copies = to_oct(lambda o: total.at[pl.ds(0, GRAD_B_TILES)], whole_b.at[own_oct], 3)
    wait_all(rank_copies)
    whole_a[own_oct] = rank_a[...]
    whole_a_copies = to_oct(lambda o: rank_a, whole_a.at[own_oct], 4)

    wait_all(oct_copies)
    n = row_places(512)
    place = (n // 128) * 128 + (n // 4 % 2) * 64 + (n // 8 % 16) * 4 + n % 4
    embeds_ref[...] = f32_dot(one_hot(place, 512), out_e[...].reshape(512, 320)).astype(
        jnp.bfloat16
    )
    wait_all(whole_b_copies)
    for o in range(OCT):
        for tile in range(GRAD_B_TILES):
            grad_b_ref[8 * o:8 * o + 8, 128 * tile:128 * tile + 128] = whole_b[o, tile]
    wait_all(whole_a_copies)
    for j in range(MP):
        for o in range(OCT):
            grad_a_ref[j, 8 * o:8 * o + 8, 0:128] = whole_a[o, j, 0]
            grad_a_ref[j, 8 * o:8 * o + 8, 128:256] = whole_a[o, j, 1]
            grad_a_ref[j, 8 * o:8 * o + 8, 256:320] = whole_a[o, j, 2][:, 0:64]

    block_copy(mine, far_send, far_recv, 0, x_next).wait_send()
    for copy in sent:
        copy.wait_send()


def local(
    patches,
    routes,
    gain,
    shift,
    first_weight,
    first_bias,
    adapter_down,
    adapter_up,
    second_weight,
    second_bias,
    language_slot_gradient,
):
    ranks = lax.axis_size("dp")
    bf16, f32 = jnp.bfloat16, jnp.float32
    destination = routes[:, 0]
    hits = (destination[:, None] == jnp.arange(ranks, dtype=jnp.int32)[None, :]).astype(jnp.int32)
    before = jnp.cumsum(hits, axis=0) - hits
    rank_in = jnp.sum(before * hits, axis=1)
    x_to, z_to, core_to = destination // 32, destination // 2 % 16, destination % 2
    place_out = z_to * 32 + x_to * 8 + core_to * 4 + rank_in
    place_in = x_to * 128 + core_to * 64 + z_to * 4 + rank_in

    rows, columns = first_weight.shape
    stacked = jnp.stack([first_weight, second_weight.T])
    stacked = jnp.pad(stacked, ((0, 0), (0, 16 - rows), (0, 0)))
    pieces = stacked.reshape(2, 16, 2, columns // 2).transpose(0, 2, 1, 3).reshape(4, 16, 640)
    down = adapter_down.reshape(4, 320, 64)

    whole = pl.BlockSpec(memory_space=pltpu.VMEM)
    semaphores = [7, 7, 8, 8, 16, 16, 8, 8, 32, 32, 15, 15, 60, 60, 35, 35]
    buffers = [
        ((64, 80, 640), bf16), ((8, 16, 640), bf16), ((4, 256, 320), bf16), ((4, 256, 320), bf16),
        ((4, 256, 320), bf16), ((2, 256, 640), bf16), ((2, 256, 640), f32), ((4, 256, 320), bf16),
        ((3, 256, 320), bf16),
        ((16, 32, 320), bf16), ((16, 32, 320), bf16), ((8, 64, 320), bf16), ((8, 64, 320), bf16),
        ((16, 32, 320), bf16), ((16, 32, 320), bf16), ((8, 64, 320), bf16), ((8, 64, 320), bf16),
        ((4, 64, 256), f32), ((8, 13, 8, 128), f32), ((8, 13, 8, 128), f32), ((16, 8, 128), f32),
        ((16, 8, 128), f32), ((16, 8, 128), f32), ((8, 10, 8, 128), f32), ((4, 3, 8, 128), f32),
        ((8, 4, 3, 8, 128), f32),
    ]
    embeds_llm, grad_a, grad_b = pl.pallas_call(
        block_kernel,
        out_shape=(
            jax.ShapeDtypeStruct((512, 320), bf16),
            jax.ShapeDtypeStruct((4, 64, 320), f32),
            jax.ShapeDtypeStruct((64, 1280), f32),
        ),
        in_specs=[whole] * 12,
        out_specs=(whole,) * 3,
        scratch_shapes=[pltpu.VMEM(shape, kind) for shape, kind in buffers]
        + [pltpu.SemaphoreType.DMA((count,)) for count in semaphores],
        compiler_params=pltpu.CompilerParams(
            collective_id=0, has_side_effects=True, vmem_limit_bytes=48 * 1024 * 1024
        ),
        name="block",
    )(
        pieces,
        patches,
        language_slot_gradient,
        place_out[None, :],
        place_in[:, None],
        gain.astype(f32).reshape(4, 1, 320),
        shift.astype(f32).reshape(4, 1, 320),
        first_bias.astype(f32).reshape(2, 1, 640),
        down,
        down.transpose(0, 2, 1),
        adapter_up.reshape(64, 2, 640).transpose(1, 0, 2),
        second_bias.astype(f32)[None, :],
    )
    return embeds_llm, grad_a.transpose(0, 2, 1).reshape(1280, 64), grad_b


def solution(mesh):
    placed = (
        P("dp", "mp"),
        P("dp", None),
        P(),
        P(),
        P("dp", "mp"),
        P("mp"),
        P(),
        P(None, "mp"),
        P("mp", "dp"),
        P("mp"),
        P("dp", "mp"),
    )
    return jax.shard_map(
        local,
        mesh=mesh,
        in_specs=placed,
        out_specs=(P("dp", "mp"), P(), P(None, "mp")),
        check_vma=False,
    )
```

time: 1170 us -> 152 us (0.13)
  waiting for transfers between devices: 1060 us -> 0 us
  Pallas kernels: 0 us -> 141 us
  starting transfers between devices: 38.3 us -> 0 us
  blocking collectives: 24.1 us -> 0 us
  between operations: 14.1 us -> 0.84 us
  matrix products: 13.2 us -> 0 us
    psum x2 -> x0, waiting for transfers between devices: 796 us -> none  [the longest x1 464 us: local(): down_gradient = lax.psum(grad_a_part, ('dp', 'mp'))]
    all_gather x2 -> x0, waiting for transfers between devices: 250 us -> none  [the longest x1 135 us: local(): lax.all_gather(second_weight, 'dp', axis=1, tiled=True)]
    pallas_call x0 -> x1, Pallas kernels: none -> 141 us  [local(): pl.pallas_call(block_kernel, out_shape=(jax.ShapeDtypeStruct((512, 320),...]
    all_to_all x2 -> x0, starting transfers between devices: 38.1 us -> none  [the longest x1 20.4 us: local(): lax.all_to_all(language_slot_gradient, 'dp', split_axis=0, concat_axis=0,...]
    all_gather x2 -> x0, blocking collectives: 24.1 us -> none  [the longest x1 12.5 us: local(): whole_rows = lax.all_gather(patches, 'mp', axis=1, tiled=True)]
    dot_general x10 -> x0, matrix products: 13.2 us -> none  [the longest x1 3.23 us: local(): lax.dot_general(whole_grad, second_full, (((1,), (1,)), ((), ())), prefer...]
  transfers between devices with their start and end apart: 7 -> 0, of which waited for: 5 -> 0; matrix products, arithmetic and copies ran while one was open for 3% -> 0% of each run, Pallas kernels for 0% -> 0%
where the time goes in v3:
time: 152 us
  Pallas kernels  141 us (93%)
  local copies, waits for them, and re-layouts  9.3 us (6%)
    pallas_call x1, Pallas kernels, local(): pl.pallas_call(block_kernel, out_shape=(jax.ShapeDtypeStruct((512, 320),...  141 us
    unnamed x28, local copies, waits for them, and re-layouts  6.86 us

profile of v3, /device:TPU:1, one launch (start us, length us, event | category | flops | bytes accessed | tf_op | source)
XLA Modules:
  0.0 151.7 jit_solution(7090648448612828530)
XLA Ops:
  0.6 0.0 copy-start.10
  0.6 0.0 copy-start.6
  0.7 0.0 copy-start.7
  0.7 0.7 copy-done.6
  1.3 0.0 copy-done.10
  1.3 0.0 copy-done.7
  1.4 0.0 copy-start.8
  1.4 0.7 copy-done.8
  2.0 0.0 copy-start.9
  2.0 0.1 reshape.243.gain_ref
  2.1 0.6 copy-done.9
  2.7 0.1 reshape.245.shift_ref
  2.8 0.2 copy.54
  3.0 0.1 copy.47
  3.1 0.2 fusion.10
  3.4 0.0 copy-start.4
  3.4 0.0 copy-start.5
  3.4 0.2 fusion.12
  3.7 0.5 copy-done.4
  4.2 0.0 copy-done.5
  4.3 0.1 copy.59
  4.4 0.1 copy.49
  4.6 0.0 copy-start.1
  4.6 0.3 fusion.6.place_col_ref
  4.8 0.7 copy-done.1
  5.5 0.0 copy-start.2
  5.5 0.9 copy-done.2
  6.4 0.2 reshape.239
  6.7 0.0 copy-start.3
  6.7 0.0 copy-start
  6.7 0.3 copy.64.down_ref
  7.0 0.6 copy-done.3
  7.6 0.2 copy.62.patches_ref
  7.8 0.0 copy-done
  7.8 0.2 copy.63.slots_ref
  8.0 140.8 %block.1 = (bf16[512,320]{1,0:T(8,128)(2,1)S(1)}, f32[4,64,320]{2,1,0:T(8,128)S(1)}, f32[64,1280]{1,0:T(8,128)S(1)}) custom-call(bf16[4,16,640]{2,1,0:T(8,128)(2,1)S(1)} %bitcast.58, bf16[256,320]{1,0:T(8,128)(2,1)S(1)} %copy.62.patches_ref, bf16[512,320]{1,0:T(8,128)(2,1)S(1)} %copy.63.slots_ref, s32[1,256]{1,0:T(1,128)S(1)} %fusion.23.place_row_ref, ...), custom_call_target="tpu_custom_call" | custom-call | tf_op jit(solution)/shard_map/block/pallas_call | solution.py:415
  148.8 0.9 copy.66
  149.7 0.3 copy.65
  150.0 1.0 reshape.241
  151.0 0.7 copy.76
  (15 shorter events, 0.2 us)
Async XLA Ops:
  0.6 0.7 copy-start.10
  0.6 0.7 copy-start.6
  0.7 0.7 copy-start.7
  1.4 0.7 copy-start.8
  2.0 0.7 copy-start.9
  3.4 0.8 copy-start.4
  3.4 0.8 copy-start.5
  4.6 0.9 copy-start.1
  5.5 0.9 copy-start.2
  6.7 0.9 copy-start.3
  6.7 1.1 copy-start

commit v4 on v3

v4 whole, which is shorter than its diff:
```python
import math

import jax
import jax.numpy as jnp
from jax import lax
from jax.experimental import pallas as pl
from jax.experimental.pallas import tpu as pltpu
from jax.sharding import PartitionSpec as P

MESH = pl.DeviceIdType.MESH
X_CHIPS, Z_CHIPS, MP = 4, 16, 4
QUAD, HALF, OCT = 4, 8, 8
MATE_LAG, NEAR_LAG, FAR_LAG = 0, 1, 2
SLOT_STEPS = {HALF - 3: [1, 2, 3, 15, 14, 13], HALF - 2: [4, 5, 12, 11], HALF - 1: [6, 7, 10, 9, 8]}
TILES, SUM_TILES = 16, 13
GRAD_B_TILES, A_TILES = 10, 3


def one_hot(places, count):
    columns = lax.broadcasted_iota(jnp.int32, (places.shape[0], count), 1)
    return (columns == places).astype(jnp.bfloat16)


def f32_dot(a, b):
    return jnp.dot(a, b, preferred_element_type=jnp.float32)


def f32_dot_t(a, b):
    return lax.dot_general(a, b, (((1,), (1,)), ((), ())), preferred_element_type=jnp.float32)


def block_kernel(
    first_hbm, second_hbm, patches_hbm, slots_hbm, routes_hbm, gain_hbm, shift_hbm,
    first_bias_hbm, second_bias_hbm, down_hbm, up_hbm,
    embeds_ref, grad_a_ref, grad_b_ref,
    shards, patches_t, slots_t, routes_ref, gain_ref, shift_ref, first_bias_ref, second_bias_ref,
    down_ref, up_ref, pieces,
    weights, staged, rows, normed, grads, act, slope, partial, got_partial,
    in_a, in_b, in_c, in_e, out_a, out_b, out_c, out_e,
    parts_b, got_b, parts_a, got_a, reduced, got_tiles, total, whole_b, whole_a,
    quad_send, quad_recv, ring_send, ring_recv, near_send, near_recv, far_send, far_recv,
    mate_send, mate_recv, y_send, y_recv, z_send, z_recv, oct_send, oct_recv,
    wide_send, wide_recv, load_sem,
):
    dp, y = lax.axis_index("dp"), lax.axis_index("mp")
    core = lax.rem(dp, 2)
    z = lax.rem(dp // 2, Z_CHIPS)
    x = dp // (2 * Z_CHIPS)
    turn = 1 - 2 * core
    own_oct = x * 2 + core

    def dp_of(x_at, z_at, core_at):
        return x_at * (2 * Z_CHIPS) + z_at * 2 + core_at

    z_turned = {d: lax.rem(z + turn * d + Z_CHIPS, Z_CHIPS) for d in range(-HALF, HALF + 1)}
    x_turned = {d: lax.rem(x + turn * d + X_CHIPS, X_CHIPS) for d in range(-2, 2)}
    x_blocks = {d: x_turned[d] * Z_CHIPS for d in x_turned}

    def block_at(x_step, z_step):
        return x_blocks[x_step] + z_turned[z_step]

    def row_places(count):
        return lax.broadcasted_iota(jnp.int32, (count, 1), 0)

    other_core = 1 - core
    cores = (core, other_core)
    lane = lax.rem(z, QUAD)
    quad_peers = []
    for step in range(QUAD):
        other = lax.rem(lane + step, QUAD)
        for flip in range(2):
            if step or flip:
                quad_peers.append((other, dp_of(x, z - lane + other, cores[flip])))
    ring_next = dp_of(x, z_turned[1], core)
    x_next = dp_of(x_turned[1], z, core)
    mate = dp_of(x, z, other_core)
    z_peers = [lax.rem(z + step, Z_CHIPS) for step in range(1, Z_CHIPS)]
    z_peer_dps = [dp_of(x, z_at, core) for z_at in z_peers]
    y_peers = [lax.rem(y + step, MP) for step in range(1, MP)]
    oct_peers = []
    for step in range(1, OCT):
        x_at, core_at = lax.rem(x + step // 2, X_CHIPS), cores[step % 2]
        oct_peers.append((x_at * 2 + core_at, dp_of(x_at, z, core_at)))

    wide_peers = []
    for y_step in range(MP):
        y_at = y_peers[y_step - 1] if y_step else y
        if y_step:
            wide_peers.append((y_at, own_oct, dp))
        wide_peers += [(y_at, at_oct, peer) for at_oct, peer in oct_peers]

    loads = [
        pltpu.make_async_copy(source, target, load_sem.at[at])
        for at, (source, target) in enumerate((
            (first_hbm, shards.at[0]), (second_hbm, shards.at[1]), (patches_hbm, patches_t),
            (slots_hbm, slots_t), (routes_hbm, routes_ref), (gain_hbm, gain_ref), (shift_hbm, shift_ref),
            (first_bias_hbm, first_bias_ref), (second_bias_hbm, second_bias_ref),
            (down_hbm, down_ref),
            (up_hbm, up_ref),
        ))
    ]
    for load in loads:
        load.start()

    barrier = pltpu.get_barrier_semaphore()
    greeted = [(peer, y) for _, peer in quad_peers]
    greeted += [(peer, y) for peer in z_peer_dps]
    greeted += [(peer, y_at) for y_at, _, peer in wide_peers]
    for peer in greeted:
        pl.semaphore_signal(barrier, inc=1, device_id=peer, device_id_type=MESH)
    for load in loads[:4]:
        load.wait()
    for weight in range(2):
        for half in range(2):
            pieces[2 * weight + half, 0:10] = shards[weight, :, 640 * half:640 * half + 640]
            pieces[2 * weight + half, 10:16] = jnp.zeros((6, 640), jnp.bfloat16)
    own_rows = f32_dot_t(one_hot(row_places(256), 256), patches_t[...]).astype(jnp.bfloat16)
    rows[y] = own_rows
    pl.semaphore_wait(barrier, len(greeted))

    sent = []

    def send(source, target, send_sem, recv_sem, peer, peer_y=None):
        copy = pltpu.make_async_remote_copy(
            src_ref=source,
            dst_ref=target,
            send_sem=send_sem,
            recv_sem=recv_sem,
            device_id=(peer, y if peer_y is None else peer_y),
            device_id_type=MESH,
        )
        copy.start()
        sent.append(copy)
        return copy

    def wait_all(copies):
        for copy in copies:
            copy.wait_recv()

    def to_y(buffer, phase):
        return [
            send(buffer.at[y], buffer.at[y], y_send.at[3 * phase + at], y_recv.at[3 * phase + at],
                 dp, y_at)
            for at, y_at in enumerate(y_peers)
        ]

    def to_one_z(source, target, phase, offset):
        z_at, at = z_peers[offset - 1], 15 * phase + offset - 1
        return send(source.at[z_at], target.at[z], z_send.at[at], z_recv.at[at],
                    z_peer_dps[offset - 1])

    def to_z(source, target, phase):
        return [to_one_z(source, target, phase, offset) for offset in range(1, Z_CHIPS)]

    def to_oct(source_of, target, phase):
        first = 7 * phase
        return [
            send(source_of(at_oct), target, oct_send.at[first + at], oct_recv.at[first + at], peer)
            for at, (at_oct, peer) in enumerate(oct_peers)
        ]

    def to_wide(source_of, target, phase):
        first = 31 * phase
        return [
            send(source_of(y_at, at_oct), target, wide_send.at[first + at],
                 wide_recv.at[first + at], peer, y_at)
            for at, (y_at, at_oct, peer) in enumerate(wide_peers)
        ]

    def block_copy(block, sends, recvs, at, peer):
        return pltpu.make_async_remote_copy(
            src_ref=weights.at[block],
            dst_ref=weights.at[block],
            send_sem=sends.at[at],
            recv_sem=recvs.at[at],
            device_id=(peer, y),
            device_id_type=MESH,
        )

    def send_block(block, sends, recvs, at, peer):
        copy = block_copy(block, sends, recvs, at, peer)
        copy.start()
        sent.append(copy)

    def arrived(block, sends, recvs, at):
        block_copy(block, sends, recvs, at, mate).wait_recv()

    def regroup_for_oct(received):
        n = row_places(512)
        place = (n // 4 % 16) * 32 + (n // 64) * 4 + n % 4
        return f32_dot(one_hot(place, 512), received[...].reshape(512, 320)).astype(
            jnp.bfloat16
        ).reshape(OCT, 64, 320)

    own = lane * 2 + core
    swaps = [
        send(pieces.at[other], staged.at[own], quad_send.at[at], quad_recv.at[at], peer)
        for at, (other, peer) in enumerate(quad_peers)
    ]
    row_copies = to_y(rows, 0)
    staged[own] = pieces[lane]

    n = row_places(512)
    place = (n // 8 % 4) * 128 + (n // 32) * 8 + n % 8
    in_a[...] = f32_dot_t(one_hot(place, 512), slots_t[...]).astype(jnp.bfloat16).reshape(
        Z_CHIPS, 32, 320
    )
    in_b[z] = in_a[z]
    slot_copies = []

    wait_all(swaps)
    n = row_places(80)
    mine = block_at(0, 0)
    weights[mine] = f32_dot(
        one_hot(n // 10 * 16 + n % 10, 128), staged[...].reshape(128, 640)
    ).astype(jnp.bfloat16)

    latents, places = [], []

    def as_row(vector):
        return vector[...].astype(jnp.float32).reshape(1, vector.shape[0])

    def down_of(j):
        return down_ref[:, 320 * j:320 * j + 320]

    def up_of(half):
        return up_ref[:, 640 * half:640 * half + 640]

    def find_places():
        at_row = lax.broadcasted_iota(jnp.int32, (256, 256), 0)
        at_column = lax.broadcasted_iota(jnp.int32, (256, 256), 1)
        wide = jnp.where(at_row == at_column, routes_ref[...], 0).astype(jnp.float32)
        routes = jnp.sum(wide, axis=1, keepdims=True).astype(jnp.int32)
        hits = one_hot(routes, 128)
        before = f32_dot((at_column < at_row).astype(jnp.bfloat16), hits)
        rank_in = jnp.sum(before * hits.astype(jnp.float32), axis=1, keepdims=True)
        rank_in = rank_in.astype(jnp.int32)
        x_to, z_to, core_to = routes // 32, routes // 2 % 16, routes % 2
        place_out = z_to * 32 + x_to * 8 + core_to * 4 + rank_in
        wide = jnp.where(at_row == at_column, place_out, 0).astype(jnp.float32)
        places.append(jnp.sum(wide, axis=0, keepdims=True).astype(jnp.int32))
        places.append(x_to * 128 + core_to * 64 + z_to * 4 + rank_in)

    def norm_rows():
        for load in loads[4:]:
            load.wait()
        find_places()
        wait_all(row_copies)
        gain, shift = as_row(gain_ref), as_row(shift_ref)
        floats = [rows[j].astype(jnp.float32) for j in range(MP)]
        mean = sum(jnp.sum(f, axis=-1, keepdims=True) for f in floats) * (1.0 / 1280)
        centred = [f - mean for f in floats]
        var = sum(jnp.sum(c * c, axis=-1, keepdims=True) for c in centred) * (1.0 / 1280)
        scale = lax.rsqrt(var + 1e-06)
        for j in range(MP):
            features = slice(320 * j, 320 * j + 320)
            normed[j] = (centred[j] * scale * gain[:, features] + shift[:, features]).astype(
                jnp.bfloat16
            )
        latents.append(
            sum(f32_dot_t(normed[j], down_of(j)) for j in range(MP)).astype(jnp.bfloat16)
        )
        latents.append(
            sum(f32_dot_t(down_of(j), normed[j]) for j in range(MP)).astype(jnp.bfloat16)
        )

    slot_steps = []

    def slots_to_oct():
        wait_all(slot_copies)
        in_c[...] = regroup_for_oct(in_b)
        in_e[own_oct] = in_c[own_oct]
        slot_steps.append(to_oct(lambda o: in_c.at[o], in_e.at[own_oct], 0))

    def pick_grads():
        wait_all(slot_steps[0])
        grads[y] = f32_dot(
            one_hot(places[1], 512), in_e[...].reshape(512, 320)
        ).astype(jnp.bfloat16)
        slot_steps.append(to_y(grads, 1))

    between = {3: [norm_rows]}

    for step in range(HALF + 1 + FAR_LAG):
        if step <= HALF:
            first = block_at(0, -step)
            if step:
                arrived(first, ring_send, ring_recv, step - 1)
            if step < HALF:
                send_block(first, ring_send, ring_recv, step, ring_next)
            send_block(first, near_send, near_recv, 2 * step if step < HALF else 15, x_next)
            if 0 < step < HALF:
                send_block(first, mate_send, mate_recv, step, mate)
        if 0 < step - MATE_LAG < HALF:
            before = step - MATE_LAG
            second = block_at(0, before)
            arrived(second, mate_send, mate_recv, before)
            send_block(second, near_send, near_recv, 2 * before - 1, x_next)
        if step in SLOT_STEPS:
            for offset in SLOT_STEPS[step]:
                slot_copies.append(to_one_z(in_a, in_b, 0, offset))
        before = step - NEAR_LAG
        if 0 <= before <= HALF:
            at = 2 * before if before < HALF else 15
            block = block_at(-1, -before)
            arrived(block, near_send, near_recv, at)
            if before == 0:
                @pl.when(core == 0)
                def _():
                    block_copy(block, far_send, far_recv, 0, x_next).start()
            elif before == HALF:
                @pl.when(core == 1)
                def _():
                    block_copy(block, far_send, far_recv, 0, x_next).start()
            else:
                send_block(block, far_send, far_recv, before, x_next)
            send_block(block, mate_send, mate_recv, 8 + at, mate)
            if 0 < before < HALF:
                block = block_at(-1, before)
                arrived(block, near_send, near_recv, 2 * before - 1)
                send_block(block, mate_send, mate_recv, 8 + 2 * before - 1, mate)
        before = step - FAR_LAG
        if 0 < before < HALF:
            block = block_at(-2, -before)
            arrived(block, far_send, far_recv, before)
            send_block(block, mate_send, mate_recv, 24 + before, mate)
        for job in between.get(step, ()):
            job()
    block = x_blocks[-2] + lax.rem(z + HALF * core, Z_CHIPS)
    arrived(block, far_send, far_recv, 0)
    send_block(block, mate_send, mate_recv, 24, mate)
    for at in range(8, 32):
        arrived(mine, mate_send, mate_recv, at)

    latent, latent_t = latents
    first_bias = as_row(first_bias_ref)

    def first_block(j, half):
        return jnp.concatenate([weights[j * 16 + quad * 4 + half] for quad in range(4)], 0)

    def second_block(j, half):
        return jnp.concatenate([weights[j * 16 + quad * 4 + 2 + half] for quad in range(4)], 0)

    for half in range(2):
        pre = sum(f32_dot(normed[j], first_block(j, half)) for j in range(MP))
        pre = pre + f32_dot(latent, up_of(half)) + first_bias[:, 640 * half:640 * half + 640]
        sigma = jax.nn.sigmoid(1.702 * pre)
        act[half] = (pre * sigma).astype(jnp.bfloat16)
        slope[half] = sigma + 1.702 * pre * sigma * (1.0 - sigma)
    partial_copies = []
    for step in (1, 2, 3, 0):
        y_at = lax.rem(y + step, MP)
        partial[step] = sum(
            f32_dot_t(act[half], second_block(y_at, half)) for half in range(2)
        ).astype(jnp.bfloat16)
        if step:
            partial_copies.append(
                send(partial.at[step], got_partial.at[step - 1], y_send.at[5 + step],
                     y_recv.at[5 + step], dp, y_at)
            )

    slots_to_oct()
    pick_grads()

    wait_all(partial_copies)
    branch = partial[0].astype(jnp.float32)
    for at in range(3):
        branch = branch + got_partial[at].astype(jnp.float32)
    embeds = (
        rows[y].astype(jnp.float32) + branch + as_row(second_bias_ref)
    ).astype(jnp.bfloat16)
    placing = (row_places(512) == places[0]).astype(jnp.bfloat16)
    out_a[...] = f32_dot(placing, embeds).astype(jnp.bfloat16).reshape(Z_CHIPS, 32, 320)
    out_b[z] = out_a[z]
    out_copies = to_z(out_a, out_b, 1)

    wait_all(slot_steps[1])
    lora_t = jnp.zeros((64, 256), jnp.float32)
    for half in range(2):
        grad_act = sum(f32_dot(grads[j], second_block(j, half)) for j in range(MP))
        grad_pre = (grad_act * slope[half]).astype(jnp.bfloat16)
        lora_t = lora_t + f32_dot_t(up_of(half), grad_pre)
        grad_b = f32_dot(latent_t, grad_pre)
        for o in range(OCT):
            for tile in range(5):
                parts_b[o, half * 5 + tile] = grad_b[8 * o:8 * o + 8, 128 * tile:128 * tile + 128]
    got_b[own_oct] = parts_b[own_oct]
    b_copies = to_oct(lambda o: parts_b.at[o], got_b.at[own_oct], 1)

    tops = []
    for _ in range(3):
        tops.append(lora_t.astype(jnp.bfloat16))
        lora_t = lora_t - tops[-1].astype(jnp.float32)
    grad_a = jnp.concatenate(
        [sum(f32_dot(top, normed[j]) for top in tops) for j in range(MP)], axis=1
    )
    for tile in range(MP * A_TILES):
        for o in range(OCT):
            strip = (
                grad_a[8 * o:8 * o + 8, 128 * tile:128 * tile + 128]
                if tile < GRAD_B_TILES
                else jnp.zeros((8, 128), jnp.float32)
            )
            parts_a[tile // A_TILES, o, tile % A_TILES] = strip
    got_a[y, own_oct] = parts_a[y, own_oct]
    a_copies = to_wide(lambda y_at, o: parts_a.at[y_at, o], got_a.at[y, own_oct], 0)

    wait_all(b_copies)
    reduced[0:GRAD_B_TILES] = jnp.sum(got_b[...], axis=0)
    wait_all(a_copies)
    reduced[GRAD_B_TILES:SUM_TILES] = jnp.sum(got_a[...], axis=(0, 1))
    reduced[SUM_TILES:TILES] = jnp.zeros((TILES - SUM_TILES, 8, 128), jnp.float32)
    got_tiles[z] = reduced[z]
    tile_copies = to_z(reduced, got_tiles, 2)

    wait_all(out_copies)
    out_c[...] = regroup_for_oct(out_b)
    out_e[own_oct] = out_c[own_oct]
    oct_copies = to_oct(lambda o: out_c.at[o], out_e.at[own_oct], 2)

    wait_all(tile_copies)
    total[z] = jnp.sum(got_tiles[...], axis=0) * (1.0 / math.sqrt(32768))
    total_copies = [
        send(total.at[z], total.at[z], z_send.at[45 + at], z_recv.at[45 + at], peer)
        for at, peer in enumerate(z_peer_dps)
    ]

    wait_all(total_copies)
    whole_b[own_oct] = total[0:GRAD_B_TILES]
    whole_b_copies = to_oct(lambda o: total.at[pl.ds(0, GRAD_B_TILES)], whole_b.at[own_oct], 3)
    whole_a[y, own_oct] = total[GRAD_B_TILES:SUM_TILES]
    whole_a_copies = to_wide(
        lambda y_at, o: total.at[pl.ds(GRAD_B_TILES, A_TILES)], whole_a.at[y, own_oct], 1
    )

    wait_all(oct_copies)
    n = row_places(512)
    place = (n // 128) * 128 + (n // 4 % 2) * 64 + (n // 8 % 16) * 4 + n % 4
    embeds_ref[...] = f32_dot(one_hot(place, 512), out_e[...].reshape(512, 320)).astype(
        jnp.bfloat16
    )
    wait_all(whole_b_copies)
    for o in range(OCT):
        for tile in range(GRAD_B_TILES):
            grad_b_ref[8 * o:8 * o + 8, 128 * tile:128 * tile + 128] = whole_b[o, tile]
    wait_all(whole_a_copies)
    for tile in range(GRAD_B_TILES):
        for o in range(OCT):
            grad_a_ref[8 * o:8 * o + 8, 128 * tile:128 * tile + 128] = whole_a[
                tile // A_TILES, o, tile % A_TILES
            ]

    block_copy(mine, far_send, far_recv, 0, x_next).wait_send()
    for copy in sent:
        copy.wait_send()


def local(
    patches,
    routes,
    gain,
    shift,
    first_weight,
    first_bias,
    adapter_down,
    adapter_up,
    second_weight,
    second_bias,
    language_slot_gradient,
):
    bf16, f32 = jnp.bfloat16, jnp.float32
    whole = pl.BlockSpec(memory_space=pltpu.VMEM)
    semaphores = [7, 7, 8, 8, 16, 16, 8, 8, 32, 32, 9, 9, 60, 60, 28, 28, 62, 62, 11]
    buffers = [
        ((2, 10, 1280), bf16), ((320, 256), bf16), ((320, 512), bf16), ((1, 256), jnp.int32),
        ((1280,), bf16), ((1280,), bf16), ((1280,), bf16), ((320,), bf16),
        ((64, 1280), bf16), ((64, 1280), bf16),
        ((4, 16, 640), bf16),
        ((64, 80, 640), bf16), ((8, 16, 640), bf16), ((4, 256, 320), bf16), ((4, 256, 320), bf16),
        ((4, 256, 320), bf16), ((2, 256, 640), bf16), ((2, 256, 640), f32), ((4, 256, 320), bf16),
        ((3, 256, 320), bf16),
        ((16, 32, 320), bf16), ((16, 32, 320), bf16), ((8, 64, 320), bf16), ((8, 64, 320), bf16),
        ((16, 32, 320), bf16), ((16, 32, 320), bf16), ((8, 64, 320), bf16), ((8, 64, 320), bf16),
        ((8, 10, 8, 128), f32), ((8, 10, 8, 128), f32), ((4, 8, 3, 8, 128), f32),
        ((4, 8, 3, 8, 128), f32), ((16, 8, 128), f32), ((16, 8, 128), f32), ((16, 8, 128), f32),
        ((8, 10, 8, 128), f32), ((4, 8, 3, 8, 128), f32),
    ]
    embeds_llm, grad_a, grad_b = pl.pallas_call(
        block_kernel,
        out_shape=(
            jax.ShapeDtypeStruct((512, 320), bf16),
            jax.ShapeDtypeStruct((64, 1280), f32),
            jax.ShapeDtypeStruct((64, 1280), f32),
        ),
        in_specs=[pl.BlockSpec(memory_space=pl.ANY)] * 11,
        out_specs=(whole,) * 3,
        scratch_shapes=[pltpu.VMEM(shape, kind) for shape, kind in buffers]
        + [pltpu.SemaphoreType.DMA((count,)) for count in semaphores],
        compiler_params=pltpu.CompilerParams(
            collective_id=0, has_side_effects=True, vmem_limit_bytes=60 * 1024 * 1024
        ),
        name="block",
    )(
        first_weight,
        second_weight.T,
        patches.T,
        language_slot_gradient.T,
        routes.T,
        gain,
        shift,
        first_bias,
        second_bias,
        adapter_down.T,
        adapter_up,
    )
    return embeds_llm, grad_a.T, grad_b


def solution(mesh):
    placed = (
        P("dp", "mp"),
        P("dp", None),
        P(),
        P(),
        P("dp", "mp"),
        P("mp"),
        P(),
        P(None, "mp"),
        P("mp", "dp"),
        P("mp"),
        P("dp", "mp"),
    )
    return jax.shard_map(
        local,
        mesh=mesh,
        in_specs=placed,
        out_specs=(P("dp", "mp"), P(), P(None, "mp")),
        check_vma=False,
    )
```

time: 152 us -> 140 us (0.921)
  Pallas kernels: 141 us -> 135 us
  local copies, waits for them, and re-layouts: 9.3 us -> 3.74 us
    pallas_call x1, Pallas kernels: 141 us -> 135 us  [local(): pl.pallas_call(block_kernel, out_shape=(jax.ShapeDtypeStruct((512, 320),...]
    unnamed x28 -> x7, local copies, waits for them, and re-layouts: 6.86 us -> 3.74 us
    reshape x8 -> x0, local copies, waits for them, and re-layouts: 1.73 us -> none  [the longest x1 1 us: local(): return (embeds_llm, grad_a.transpose(0, 2, 1).reshape(1280, 64), grad_b)]
where the time goes in v4:
time: 140 us; the launch traced here: 139 us
  Pallas kernels  135 us (96%)
  local copies, waits for them, and re-layouts  3.74 us (3%)
    pallas_call x1, Pallas kernels, local(): pl.pallas_call(block_kernel, out_shape=(jax.ShapeDtypeStruct((512, 320),...  135 us
    unnamed x7, local copies, waits for them, and re-layouts  3.74 us

profile of v4, /device:TPU:1, one launch (start us, length us, event | category | flops | bytes accessed | tf_op | source)
XLA Modules:
  0.0 139.4 jit_solution(5525833711458008185)
XLA Ops:
  0.6 135.0 %block.1 = (bf16[512,320]{1,0:T(8,128)(2,1)}, f32[64,1280]{1,0:T(8,128)}, f32[64,1280]{1,0:T(8,128)}) custom-call(bf16[10,1280]{1,0:T(8,128)(2,1)} %first_hbm.1, bf16[10,1280]{1,0:T(8,128)(2,1)} %bitcast.10, bf16[320,256]{1,0:T(8,128)(2,1)} %bitcast.8, bf16[320,512]{1,0:T(8,128)(2,1)} %bitcast.6, s32[1,256]{1,0:T(1,128)} %bitcast.11, ...), custom_call_target="tpu_custom_call" | custom-call | tf_op jit(solution)/shard_map/block/pallas_call | solution.py:488
  135.7 0.0 copy-start.1
  135.7 1.9 %copy.14 = bf16[512,320]{0,1:T(8,128)(2,1)} copy(bf16[512,320]{1,0:T(8,128)(2,1)} %get-tuple-element.9) | data formatting | bytes 655360
  137.6 0.0 copy-done.1
  137.6 0.0 copy-start
  137.6 0.7 copy.17
  138.3 0.4 copy-done
  138.7 0.7 copy.18
Async XLA Ops:
  135.7 1.9 %copy-start.1 = (f32[64,1280]{1,0:T(8,128)S(1)}, f32[64,1280]{1,0:T(8,128)}, u32[]{:S(2)}) copy-start(f32[64,1280]{1,0:T(8,128)} %get-tuple-element.7) | copy-start | bytes 983044
  137.6 1.1 copy-start

commit v5 on v4

--- a/solution.py
+++ b/solution.py
@@ -27,6 +27,22 @@
 
 def f32_dot_t(a, b):
     return lax.dot_general(a, b, (((1,), (1,)), ((), ())), preferred_element_type=jnp.float32)
+
+
+def pack(values, groups):
+    values = values.reshape(groups, -1, 320)
+    half = values.shape[1] // 2
+    tail = jnp.concatenate([values[:, :half, 256:320], values[:, half:, 256:320]], axis=2)
+    return jnp.concatenate([values[:, :, 0:128], values[:, :, 128:256], tail], axis=1)
+
+
+def unpack(packed):
+    groups, count = packed.shape[0], packed.shape[1] * 2 // 5
+    tail = packed[:, 2 * count:]
+    tail = jnp.concatenate([tail[:, :, 0:64], tail[:, :, 64:128]], axis=1)
+    return jnp.concatenate(
+        [packed[:, :count], packed[:, count:2 * count], tail], axis=2
+    ).reshape(groups * count, 320)
 
 
 def block_kernel(
@@ -114,8 +130,7 @@
         for half in range(2):
             pieces[2 * weight + half, 0:10] = shards[weight, :, 640 * half:640 * half + 640]
             pieces[2 * weight + half, 10:16] = jnp.zeros((6, 640), jnp.bfloat16)
-    own_rows = f32_dot_t(one_hot(row_places(256), 256), patches_t[...]).astype(jnp.bfloat16)
-    rows[y] = own_rows
+    rows[y] = patches_t[...]
     pl.semaphore_wait(barrier, len(greeted))
 
     sent = []
@@ -188,9 +203,8 @@
     def regroup_for_oct(received):
         n = row_places(512)
         place = (n // 4 % 16) * 32 + (n // 64) * 4 + n % 4
-        return f32_dot(one_hot(place, 512), received[...].reshape(512, 320)).astype(
-            jnp.bfloat16
-        ).reshape(OCT, 64, 320)
+        moved = f32_dot(one_hot(place, 512), unpack(received[...]))
+        return pack(moved.astype(jnp.bfloat16), OCT)
 
     own = lane * 2 + core
     swaps = [
@@ -202,9 +216,8 @@
 
     n = row_places(512)
     place = (n // 8 % 4) * 128 + (n // 32) * 8 + n % 8
-    in_a[...] = f32_dot_t(one_hot(place, 512), slots_t[...]).astype(jnp.bfloat16).reshape(
-        Z_CHIPS, 32, 320
-    )
+    moved = f32_dot_t(one_hot(place, 512), slots_t[...])
+    in_a[...] = pack(moved.astype(jnp.bfloat16), Z_CHIPS)
     in_b[z] = in_a[z]
     slot_copies = []
 
@@ -216,6 +229,7 @@
     ).astype(jnp.bfloat16)
 
     latents, places = [], []
+    same = one_hot(row_places(256), 256)
 
     def as_row(vector):
         return vector[...].astype(jnp.float32).reshape(1, vector.shape[0])
@@ -247,7 +261,7 @@
         find_places()
         wait_all(row_copies)
         gain, shift = as_row(gain_ref), as_row(shift_ref)
-        floats = [rows[j].astype(jnp.float32) for j in range(MP)]
+        floats = [f32_dot_t(same, rows[j]) for j in range(MP)]
         mean = sum(jnp.sum(f, axis=-1, keepdims=True) for f in floats) * (1.0 / 1280)
         centred = [f - mean for f in floats]
         var = sum(jnp.sum(c * c, axis=-1, keepdims=True) for c in centred) * (1.0 / 1280)
@@ -274,9 +288,8 @@
 
     def pick_grads():
         wait_all(slot_steps[0])
-        grads[y] = f32_dot(
-            one_hot(places[1], 512), in_e[...].reshape(512, 320)
-        ).astype(jnp.bfloat16)
+        picked = f32_dot(one_hot(places[1], 512), unpack(in_e[...])).astype(jnp.bfloat16)
+        grads[y] = f32_dot_t(one_hot(row_places(320), 320), picked).astype(jnp.bfloat16)
         slot_steps.append(to_y(grads, 1))
 
     between = {3: [norm_rows]}
@@ -351,7 +364,7 @@
     for step in (1, 2, 3, 0):
         y_at = lax.rem(y + step, MP)
         partial[step] = sum(
-            f32_dot_t(act[half], second_block(y_at, half)) for half in range(2)
+            f32_dot_t(second_block(y_at, half), act[half]) for half in range(2)
         ).astype(jnp.bfloat16)
         if step:
             partial_copies.append(
@@ -366,18 +379,22 @@
     branch = partial[0].astype(jnp.float32)
     for at in range(3):
         branch = branch + got_partial[at].astype(jnp.float32)
-    embeds = (
-        rows[y].astype(jnp.float32) + branch + as_row(second_bias_ref)
-    ).astype(jnp.bfloat16)
+    at_row = lax.broadcasted_iota(jnp.int32, (320, 320), 0)
+    at_column = lax.broadcasted_iota(jnp.int32, (320, 320), 1)
+    bias = jnp.sum(
+        jnp.where(at_row == at_column, as_row(second_bias_ref), 0.0), axis=1, keepdims=True
+    )
+    embeds = (patches_t[...].astype(jnp.float32) + branch + bias).astype(jnp.bfloat16)
     placing = (row_places(512) == places[0]).astype(jnp.bfloat16)
-    out_a[...] = f32_dot(placing, embeds).astype(jnp.bfloat16).reshape(Z_CHIPS, 32, 320)
+    out_a[...] = pack(f32_dot_t(placing, embeds).astype(jnp.bfloat16), Z_CHIPS)
     out_b[z] = out_a[z]
     out_copies = to_z(out_a, out_b, 1)
 
     wait_all(slot_steps[1])
+    grad_rows = [f32_dot_t(same, grads[j]).astype(jnp.bfloat16) for j in range(MP)]
     lora_t = jnp.zeros((64, 256), jnp.float32)
     for half in range(2):
-        grad_act = sum(f32_dot(grads[j], second_block(j, half)) for j in range(MP))
+        grad_act = sum(f32_dot(grad_rows[j], second_block(j, half)) for j in range(MP))
         grad_pre = (grad_act * slope[half]).astype(jnp.bfloat16)
         lora_t = lora_t + f32_dot_t(up_of(half), grad_pre)
         grad_b = f32_dot(latent_t, grad_pre)
@@ -436,9 +453,7 @@
     wait_all(oct_copies)
     n = row_places(512)
     place = (n // 128) * 128 + (n // 4 % 2) * 64 + (n // 8 % 16) * 4 + n % 4
-    embeds_ref[...] = f32_dot(one_hot(place, 512), out_e[...].reshape(512, 320)).astype(
-        jnp.bfloat16
-    )
+    embeds_ref[...] = f32_dot(one_hot(place, 512), unpack(out_e[...])).T.astype(jnp.bfloat16)
     wait_all(whole_b_copies)
     for o in range(OCT):
         for tile in range(GRAD_B_TILES):
@@ -476,11 +491,11 @@
         ((1280,), bf16), ((1280,), bf16), ((1280,), bf16), ((320,), bf16),
         ((64, 1280), bf16), ((64, 1280), bf16),
         ((4, 16, 640), bf16),
-        ((64, 80, 640), bf16), ((8, 16, 640), bf16), ((4, 256, 320), bf16), ((4, 256, 320), bf16),
-        ((4, 256, 320), bf16), ((2, 256, 640), bf16), ((2, 256, 640), f32), ((4, 256, 320), bf16),
-        ((3, 256, 320), bf16),
-        ((16, 32, 320), bf16), ((16, 32, 320), bf16), ((8, 64, 320), bf16), ((8, 64, 320), bf16),
-        ((16, 32, 320), bf16), ((16, 32, 320), bf16), ((8, 64, 320), bf16), ((8, 64, 320), bf16),
+        ((64, 80, 640), bf16), ((8, 16, 640), bf16), ((4, 320, 256), bf16), ((4, 256, 320), bf16),
+        ((4, 320, 256), bf16), ((2, 256, 640), bf16), ((2, 256, 640), f32), ((4, 320, 256), bf16),
+        ((3, 320, 256), bf16),
+        ((16, 80, 128), bf16), ((16, 80, 128), bf16), ((8, 160, 128), bf16), ((8, 160, 128), bf16),
+        ((16, 80, 128), bf16), ((16, 80, 128), bf16), ((8, 160, 128), bf16), ((8, 160, 128), bf16),
         ((8, 10, 8, 128), f32), ((8, 10, 8, 128), f32), ((4, 8, 3, 8, 128), f32),
         ((4, 8, 3, 8, 128), f32), ((16, 8, 128), f32), ((16, 8, 128), f32), ((16, 8, 128), f32),
         ((8, 10, 8, 128), f32), ((4, 8, 3, 8, 128), f32),
@@ -488,7 +503,7 @@
     embeds_llm, grad_a, grad_b = pl.pallas_call(
         block_kernel,
         out_shape=(
-            jax.ShapeDtypeStruct((512, 320), bf16),
+            jax.ShapeDtypeStruct((320, 512), bf16),
             jax.ShapeDtypeStruct((64, 1280), f32),
             jax.ShapeDtypeStruct((64, 1280), f32),
         ),
@@ -513,7 +528,7 @@
         adapter_down.T,
         adapter_up,
     )
-    return embeds_llm, grad_a.T, grad_b
+    return embeds_llm.T, grad_a.T, grad_b
 
 
 def solution(mesh):

time: 140 us -> 135 us (0.964)
  Pallas kernels: 135 us -> 130 us
    pallas_call x1, Pallas kernels: 135 us -> 130 us  [local(): pl.pallas_call(block_kernel, out_shape=(jax.ShapeDtypeStruct((320, 512),...]
where the time goes in v5:
time: 135 us
  Pallas kernels  130 us (96%)
  local copies, waits for them, and re-layouts  3.58 us (3%)
    pallas_call x1, Pallas kernels, local(): pl.pallas_call(block_kernel, out_shape=(jax.ShapeDtypeStruct((320, 512),...  130 us
    unnamed x7, local copies, waits for them, and re-layouts  3.58 us

profile of v5, /device:TPU:1, one launch (start us, length us, event | category | flops | bytes accessed | tf_op | source)
XLA Modules:
  0.0 134.5 jit_solution(16461743680840842123)
XLA Ops:
  0.6 130.3 %block.1 = (bf16[320,512]{1,0:T(8,128)(2,1)}, f32[64,1280]{1,0:T(8,128)}, f32[64,1280]{1,0:T(8,128)}) custom-call(bf16[10,1280]{1,0:T(8,128)(2,1)} %first_hbm.1, bf16[10,1280]{1,0:T(8,128)(2,1)} %bitcast.12, bf16[320,256]{1,0:T(8,128)(2,1)} %bitcast.10, bf16[320,512]{1,0:T(8,128)(2,1)} %bitcast.7, s32[1,256]{1,0:T(1,128)} %bitcast.13, ...), custom_call_target="tpu_custom_call" | custom-call | tf_op jit(solution)/shard_map/block/pallas_call | solution.py:503
  131.0 0.0 copy-start.1
  131.0 1.8 %copy.17 = bf16[512,320]{0,1:T(8,128)(2,1)} copy(bf16[512,320]{0,1:T(8,128)(2,1)} %bitcast.9) | data formatting | bytes 655360
  132.7 0.0 copy-done.1
  132.7 0.0 copy-start
  132.7 0.7 copy.18
  133.5 0.4 copy-done
  133.8 0.7 copy.19
Async XLA Ops:
  131.0 1.8 %copy-start.1 = (f32[64,1280]{1,0:T(8,128)S(1)}, f32[64,1280]{1,0:T(8,128)}, u32[]{:S(2)}) copy-start(f32[64,1280]{1,0:T(8,128)} %get-tuple-element.7) | copy-start | bytes 983044
  132.7 1.1 copy-start

commit v6 on v5

--- a/solution.py
+++ b/solution.py
@@ -14,6 +14,7 @@
 SLOT_STEPS = {HALF - 3: [1, 2, 3, 15, 14, 13], HALF - 2: [4, 5, 12, 11], HALF - 1: [6, 7, 10, 9, 8]}
 TILES, SUM_TILES = 16, 13
 GRAD_B_TILES, A_TILES = 10, 3
+FAR_FIRST = sorted(range(1, Z_CHIPS), key=lambda offset: abs(offset - HALF))
 
 
 def one_hot(places, count):
@@ -54,9 +55,10 @@
     weights, staged, rows, normed, grads, act, slope, partial, got_partial,
     in_a, in_b, in_c, in_e, out_a, out_b, out_c, out_e,
     parts_b, got_b, parts_a, got_a, reduced, got_tiles, total, whole_b, whole_a,
+    regroup, ordered, placing, picking, same_features,
     quad_send, quad_recv, ring_send, ring_recv, near_send, near_recv, far_send, far_recv,
     mate_send, mate_recv, y_send, y_recv, z_send, z_recv, oct_send, oct_recv,
-    wide_send, wide_recv, load_sem,
+    wide_send, wide_recv, end_send, end_recv, load_sem,
 ):
     dp, y = lax.axis_index("dp"), lax.axis_index("mp")
     core = lax.rem(dp, 2)
@@ -105,6 +107,11 @@
             wide_peers.append((y_at, own_oct, dp))
         wide_peers += [(y_at, at_oct, peer) for at_oct, peer in oct_peers]
 
+    x_peers = [lax.rem(x + step, X_CHIPS) for step in range(1, X_CHIPS)]
+    x_peer_dps = [dp_of(x_at, z, core) for x_at in x_peers]
+    plane_peers = [(y, peer) for peer in x_peer_dps]
+    plane_peers += [(y_at, peer) for y_at in y_peers for peer in [dp] + x_peer_dps]
+
     loads = [
         pltpu.make_async_copy(source, target, load_sem.at[at])
         for at, (source, target) in enumerate((
@@ -165,7 +172,7 @@
                     z_peer_dps[offset - 1])
 
     def to_z(source, target, phase):
-        return [to_one_z(source, target, phase, offset) for offset in range(1, Z_CHIPS)]
+        return [to_one_z(source, target, phase, offset) for offset in FAR_FIRST]
 
     def to_oct(source_of, target, phase):
         first = 7 * phase
@@ -201,9 +208,7 @@
         block_copy(block, sends, recvs, at, mate).wait_recv()
 
     def regroup_for_oct(received):
-        n = row_places(512)
-        place = (n // 4 % 16) * 32 + (n // 64) * 4 + n % 4
-        moved = f32_dot(one_hot(place, 512), unpack(received[...]))
+        moved = f32_dot(regroup[...], unpack(received[...]))
         return pack(moved.astype(jnp.bfloat16), OCT)
 
     own = lane * 2 + core
@@ -280,6 +285,16 @@
 
     slot_steps = []
 
+    def make_moves():
+        n = row_places(512)
+        regroup[...] = one_hot((n // 4 % 16) * 32 + (n // 64) * 4 + n % 4, 512)
+        ordered[...] = one_hot(
+            (n // 128) * 128 + (n // 4 % 2) * 64 + (n // 8 % 16) * 4 + n % 4, 512
+        )
+        placing[...] = (n == places[0]).astype(jnp.bfloat16)
+        picking[...] = one_hot(places[1], 512)
+        same_features[...] = one_hot(row_places(320), 320)
+
     def slots_to_oct():
         wait_all(slot_copies)
         in_c[...] = regroup_for_oct(in_b)
@@ -288,11 +303,11 @@
 
     def pick_grads():
         wait_all(slot_steps[0])
-        picked = f32_dot(one_hot(places[1], 512), unpack(in_e[...])).astype(jnp.bfloat16)
-        grads[y] = f32_dot_t(one_hot(row_places(320), 320), picked).astype(jnp.bfloat16)
+        picked = f32_dot(picking[...], unpack(in_e[...])).astype(jnp.bfloat16)
+        grads[y] = f32_dot_t(same_features[...], picked).astype(jnp.bfloat16)
         slot_steps.append(to_y(grads, 1))
 
-    between = {3: [norm_rows]}
+    between = {3: [norm_rows], 6: [make_moves]}
 
     for step in range(HALF + 1 + FAR_LAG):
         if step <= HALF:
@@ -361,7 +376,7 @@
         act[half] = (pre * sigma).astype(jnp.bfloat16)
         slope[half] = sigma + 1.702 * pre * sigma * (1.0 - sigma)
     partial_copies = []
-    for step in (1, 2, 3, 0):
+    for step in (2, 1, 3, 0):
         y_at = lax.rem(y + step, MP)
         partial[step] = sum(
             f32_dot_t(second_block(y_at, half), act[half]) for half in range(2)
@@ -385,8 +400,7 @@
         jnp.where(at_row == at_column, as_row(second_bias_ref), 0.0), axis=1, keepdims=True
     )
     embeds = (patches_t[...].astype(jnp.float32) + branch + bias).astype(jnp.bfloat16)
-    placing = (row_places(512) == places[0]).astype(jnp.bfloat16)
-    out_a[...] = pack(f32_dot_t(placing, embeds).astype(jnp.bfloat16), Z_CHIPS)
+    out_a[...] = pack(f32_dot_t(placing[...], embeds).astype(jnp.bfloat16), Z_CHIPS)
     out_b[z] = out_a[z]
     out_copies = to_z(out_a, out_b, 1)
 
@@ -439,30 +453,40 @@
     total[z] = jnp.sum(got_tiles[...], axis=0) * (1.0 / math.sqrt(32768))
     total_copies = [
         send(total.at[z], total.at[z], z_send.at[45 + at], z_recv.at[45 + at], peer)
-        for at, peer in enumerate(z_peer_dps)
+        for at, peer in ((offset - 1, z_peer_dps[offset - 1]) for offset in FAR_FIRST)
     ]
 
     wait_all(total_copies)
-    whole_b[own_oct] = total[0:GRAD_B_TILES]
-    whole_b_copies = to_oct(lambda o: total.at[pl.ds(0, GRAD_B_TILES)], whole_b.at[own_oct], 3)
-    whole_a[y, own_oct] = total[GRAD_B_TILES:SUM_TILES]
-    whole_a_copies = to_wide(
-        lambda y_at, o: total.at[pl.ds(GRAD_B_TILES, A_TILES)], whole_a.at[y, own_oct], 1
-    )
-
+    whole_b[core, x] = total[0:GRAD_B_TILES]
+    whole_a[core, y, x] = total[GRAD_B_TILES:SUM_TILES]
+    b_target, a_target = whole_b.at[core, x], whole_a.at[core, y, x]
+    whole_copies = [
+        send(total.at[pl.ds(0, GRAD_B_TILES)], b_target, end_send.at[at], end_recv.at[at], peer)
+        for at, peer in enumerate(x_peer_dps)
+    ]
+    whole_copies += [
+        send(total.at[pl.ds(GRAD_B_TILES, A_TILES)], a_target, end_send.at[3 + at],
+             end_recv.at[3 + at], peer, y_at)
+        for at, (y_at, peer) in enumerate(plane_peers)
+    ]
+
+    wait_all(whole_copies)
+    mate_copies = [
+        send(whole.at[core], whole.at[core], end_send.at[18 + at], end_recv.at[18 + at], mate)
+        for at, whole in enumerate((whole_b, whole_a))
+    ]
     wait_all(oct_copies)
-    n = row_places(512)
-    place = (n // 128) * 128 + (n // 4 % 2) * 64 + (n // 8 % 16) * 4 + n % 4
-    embeds_ref[...] = f32_dot(one_hot(place, 512), unpack(out_e[...])).T.astype(jnp.bfloat16)
-    wait_all(whole_b_copies)
+    embeds_ref[...] = f32_dot(ordered[...], unpack(out_e[...])).T.astype(jnp.bfloat16)
+    wait_all(mate_copies)
     for o in range(OCT):
         for tile in range(GRAD_B_TILES):
-            grad_b_ref[8 * o:8 * o + 8, 128 * tile:128 * tile + 128] = whole_b[o, tile]
-    wait_all(whole_a_copies)
+            grad_b_ref[8 * o:8 * o + 8, 128 * tile:128 * tile + 128] = whole_b[
+                o % 2, o // 2, tile
+            ]
     for tile in range(GRAD_B_TILES):
         for o in range(OCT):
             grad_a_ref[8 * o:8 * o + 8, 128 * tile:128 * tile + 128] = whole_a[
-                tile // A_TILES, o, tile % A_TILES
+                o % 2, tile // A_TILES, o // 2, tile % A_TILES
             ]
 
     block_copy(mine, far_send, far_recv, 0, x_next).wait_send()
@@ -485,7 +509,7 @@
 ):
     bf16, f32 = jnp.bfloat16, jnp.float32
     whole = pl.BlockSpec(memory_space=pltpu.VMEM)
-    semaphores = [7, 7, 8, 8, 16, 16, 8, 8, 32, 32, 9, 9, 60, 60, 28, 28, 62, 62, 11]
+    semaphores = [7, 7, 8, 8, 16, 16, 8, 8, 32, 32, 9, 9, 60, 60, 21, 21, 31, 31, 20, 20, 11]
     buffers = [
         ((2, 10, 1280), bf16), ((320, 256), bf16), ((320, 512), bf16), ((1, 256), jnp.int32),
         ((1280,), bf16), ((1280,), bf16), ((1280,), bf16), ((320,), bf16),
@@ -498,7 +522,9 @@
         ((16, 80, 128), bf16), ((16, 80, 128), bf16), ((8, 160, 128), bf16), ((8, 160, 128), bf16),
         ((8, 10, 8, 128), f32), ((8, 10, 8, 128), f32), ((4, 8, 3, 8, 128), f32),
         ((4, 8, 3, 8, 128), f32), ((16, 8, 128), f32), ((16, 8, 128), f32), ((16, 8, 128), f32),
-        ((8, 10, 8, 128), f32), ((4, 8, 3, 8, 128), f32),
+        ((2, 4, 10, 8, 128), f32), ((2, 4, 4, 3, 8, 128), f32),
+        ((512, 512), bf16), ((512, 512), bf16), ((512, 256), bf16), ((256, 512), bf16),
+        ((320, 320), bf16),
     ]
     embeds_llm, grad_a, grad_b = pl.pallas_call(
         block_kernel,

time: 135 us -> 132 us (0.978)
  Pallas kernels: 130 us -> 128 us
    pallas_call x1, Pallas kernels: 130 us -> 128 us  [local(): pl.pallas_call(block_kernel, out_shape=(jax.ShapeDtypeStruct((320, 512),...]
where the time goes in v6:
time: 132 us
  Pallas kernels  128 us (97%)
  local copies, waits for them, and re-layouts  3.58 us (3%)
    pallas_call x1, Pallas kernels, local(): pl.pallas_call(block_kernel, out_shape=(jax.ShapeDtypeStruct((320, 512),...  128 us
    unnamed x7, local copies, waits for them, and re-layouts  3.58 us

profile of v6, /device:TPU:1, one launch (start us, length us, event | category | flops | bytes accessed | tf_op | source)
XLA Modules:
  0.0 131.9 jit_solution(48463181796571820)
XLA Ops:
  0.6 127.7 %block.1 = (bf16[320,512]{1,0:T(8,128)(2,1)}, f32[64,1280]{1,0:T(8,128)}, f32[64,1280]{1,0:T(8,128)}) custom-call(bf16[10,1280]{1,0:T(8,128)(2,1)} %first_hbm.1, bf16[10,1280]{1,0:T(8,128)(2,1)} %bitcast.12, bf16[320,256]{1,0:T(8,128)(2,1)} %bitcast.10, bf16[320,512]{1,0:T(8,128)(2,1)} %bitcast.7, s32[1,256]{1,0:T(1,128)} %bitcast.13, ...), custom_call_target="tpu_custom_call" | custom-call | tf_op jit(solution)/shard_map/block/pallas_call | solution.py:529
  128.3 0.0 copy-start.1
  128.3 1.8 %copy.17 = bf16[512,320]{0,1:T(8,128)(2,1)} copy(bf16[512,320]{0,1:T(8,128)(2,1)} %bitcast.9) | data formatting | bytes 655360
  130.1 0.0 copy-done.1
  130.1 0.0 copy-start
  130.1 0.7 copy.18
  130.8 0.4 copy-done
  131.2 0.7 copy.19
Async XLA Ops:
  128.3 1.8 %copy-start.1 = (f32[64,1280]{1,0:T(8,128)S(1)}, f32[64,1280]{1,0:T(8,128)}, u32[]{:S(2)}) copy-start(f32[64,1280]{1,0:T(8,128)} %get-tuple-element.7) | copy-start | bytes 983044
  130.1 1.1 copy-start

commit v7 on v6

--- a/solution.py
+++ b/solution.py
@@ -201,6 +201,22 @@
 
     def send_block(block, sends, recvs, at, peer):
         copy = block_copy(block, sends, recvs, at, peer)
+        copy.start()
+        sent.append(copy)
+
+    def ring_part(block, part, step):
+        rows_of = pl.ds(48 * part, 48 - 16 * part)
+        return pltpu.make_async_remote_copy(
+            src_ref=weights.at[block, rows_of],
+            dst_ref=weights.at[block, rows_of],
+            send_sem=ring_send.at[2 * step + part],
+            recv_sem=ring_recv.at[2 * step + part],
+            device_id=(ring_next, y),
+            device_id_type=MESH,
+        )
+
+    def send_ring_part(block, part, step):
+        copy = ring_part(block, part, step)
         copy.start()
         sent.append(copy)
 
@@ -313,9 +329,13 @@
         if step <= HALF:
             first = block_at(0, -step)
             if step:
-                arrived(first, ring_send, ring_recv, step - 1)
-            if step < HALF:
-                send_block(first, ring_send, ring_recv, step, ring_next)
+                for part in range(2):
+                    ring_part(first, part, step - 1).wait_recv()
+                    if step < HALF:
+                        send_ring_part(first, part, step)
+            else:
+                send_ring_part(first, 0, step)
+                send_ring_part(first, 1, step)
             send_block(first, near_send, near_recv, 2 * step if step < HALF else 15, x_next)
             if 0 < step < HALF:
                 send_block(first, mate_send, mate_recv, step, mate)
@@ -509,7 +529,7 @@
 ):
     bf16, f32 = jnp.bfloat16, jnp.float32
     whole = pl.BlockSpec(memory_space=pltpu.VMEM)
-    semaphores = [7, 7, 8, 8, 16, 16, 8, 8, 32, 32, 9, 9, 60, 60, 21, 21, 31, 31, 20, 20, 11]
+    semaphores = [7, 7, 16, 16, 16, 16, 8, 8, 32, 32, 9, 9, 60, 60, 21, 21, 31, 31, 20, 20, 11]
     buffers = [
         ((2, 10, 1280), bf16), ((320, 256), bf16), ((320, 512), bf16), ((1, 256), jnp.int32),
         ((1280,), bf16), ((1280,), bf16), ((1280,), bf16), ((320,), bf16),

time: 132 us -> 132 us (level)
  no operation moved by 1% of the time
where the time goes in v7:
time: 132 us; the launch traced here: 131 us
  Pallas kernels  127 us (96%)
  local copies, waits for them, and re-layouts  3.58 us (3%)
    pallas_call x1, Pallas kernels, local(): pl.pallas_call(block_kernel, out_shape=(jax.ShapeDtypeStruct((320, 512),...  127 us
    unnamed x7, local copies, waits for them, and re-layouts  3.58 us

profile of v7, /device:TPU:1, one launch (start us, length us, event | category | flops | bytes accessed | tf_op | source)
XLA Modules:
  0.0 131.4 jit_solution(12186385340085135730)
XLA Ops:
  0.6 127.2 %block.1 = (bf16[320,512]{1,0:T(8,128)(2,1)}, f32[64,1280]{1,0:T(8,128)}, f32[64,1280]{1,0:T(8,128)}) custom-call(bf16[10,1280]{1,0:T(8,128)(2,1)} %first_hbm.1, bf16[10,1280]{1,0:T(8,128)(2,1)} %bitcast.12, bf16[320,256]{1,0:T(8,128)(2,1)} %bitcast.10, bf16[320,512]{1,0:T(8,128)(2,1)} %bitcast.7, s32[1,256]{1,0:T(1,128)} %bitcast.13, ...), custom_call_target="tpu_custom_call" | custom-call | tf_op jit(solution)/shard_map/block/pallas_call | solution.py:549
  127.8 0.0 copy-start.1
  127.8 1.8 %copy.17 = bf16[512,320]{0,1:T(8,128)(2,1)} copy(bf16[512,320]{0,1:T(8,128)(2,1)} %bitcast.9) | data formatting | bytes 655360
  129.6 0.0 copy-done.1
  129.6 0.0 copy-start
  129.6 0.7 copy.18
  130.3 0.4 copy-done
  130.7 0.7 copy.19
Async XLA Ops:
  127.8 1.8 %copy-start.1 = (f32[64,1280]{1,0:T(8,128)S(1)}, f32[64,1280]{1,0:T(8,128)}, u32[]{:S(2)}) copy-start(f32[64,1280]{1,0:T(8,128)} %get-tuple-element.7) | copy-start | bytes 983044
  129.6 1.1 copy-start
